TPU v7x, 512 devices: a whole 4x4x16 slice. The times are simulated.
512 devices in a mesh: blk: 128 (over x_hi, y, z), grp: 4 (over x_lo, core).
Axes of the slice: x: 4 (x_hi: 2, x_lo: 2; x = x_hi * 2 + x_lo), y: 4, z: 16, core: 2. Of those that a mesh axis runs over, the one named last changes fastest.
Arguments:
- image_emb: bfloat16 [196608, 1152], P(('blk', 'grp')), may hold values from -0.1875 to 0.1875
- text_emb: bfloat16 [196608, 1152], P(('blk', 'grp')), may hold values from -0.1875 to 0.1875
- positives: int32 [512, 384], P(('blk', 'grp')), may hold values from 0 to 383, each once within a row
- pair_mask: int32 [128, 7], replicated, may hold values from 0 to 1, as said below
- log_scale: float32 [1], replicated, may hold values from 1.5 to 2.5
- bias: float32 [1], replicated, may hold values from -3 to -1
Outputs:
- image_grad: bfloat16 [196608, 1152], P(('blk', 'grp'))
- text_grad: bfloat16 [196608, 1152], P(('blk', 'grp'))
- loss: float32 [1], replicated
Inputs may be any that keep to these rules, and one draw needn't show every extreme that they name: `positives`: every row is a permutation of the rows of a block. `pair_mask`: column 3 is 1 in every row (each image block is scored against its own text block); at least one row is all ones.
All inputs are finite; a program needn't handle non-finite values.
Results may differ from a plain program's by a relative error of at most 0.0063.
Values may be sent and summed in bfloat16 or wider, within the bound.
No kernel may reach another device: no remote copies, remote signals or barrier semaphores. Data moves between devices by JAX's collectives and lax.ppermute only.
A program may use at most 64 MiB of HBM per device.

v0:
```python
import functools

import jax
import jax.numpy as jnp
from jax import lax
from jax.sharding import Mesh
from jax.sharding import PartitionSpec as P

BLK = ("blk_0", "blk_1", "blk_2")
BLK_GRP = ("blk_0", "blk_1", "blk_2", "grp_0", "grp_1")
GRP = ("grp_0", "grp_1")


epsilon = 1e-06


def passed_along(value, axis, steps):
    count = lax.axis_size(axis)
    pairs = [(source, (source + steps) % count) for source in range(count)]
    return lax.ppermute(value, axis, pairs)


def by_axis(shard, axes):
    return functools.reduce(lax.psum, axes, shard)


def unit_rows(embedded):
    values = embedded.astype(jnp.float32)
    length = jnp.sqrt(jnp.sum(values * values, axis=1, keepdims=True) + epsilon)
    return (values / length, length)


def back_rows(normed, length, upstream):
    inward = jnp.sum(normed * upstream, axis=1, keepdims=True)
    return (upstream - normed * inward) / length


def score_tile(image_side, text_side, labels, logit_scale, offset):
    similar = jnp.einsum("rd,cd->rc", image_side, text_side, preferred_element_type=jnp.float32)
    logits = logit_scale * similar + offset
    signed = labels * logits
    loss_sum = jnp.sum(jax.nn.softplus(-signed))
    slopes = (-labels * jax.nn.sigmoid(-signed) * logit_scale).astype(jnp.bfloat16)
    return (slopes, loss_sum)


def masked_tile(active_flag, image_side, text_side, labels, logit_scale, offset):

    def active(unused):
        return score_tile(image_side, text_side, labels, logit_scale, offset)

    def skipped(unused):
        return (
            jnp.zeros((image_side.shape[0], text_side.shape[0]), jnp.bfloat16),
            jnp.zeros((), jnp.float32),
        )

    return lax.cond(active_flag > 0, active, skipped, 0)


def body(image_emb, text_emb, positives, pair_mask, log_scale, bias):
    reach = (pair_mask.shape[1] - 1) // 2
    block_count = lax.axis_size(BLK)
    myself = lax.axis_index(BLK)
    logit_scale = jnp.exp(log_scale[0])
    offset = bias[0]
    row_count = image_emb.shape[0]
    image_normed, image_len = unit_rows(image_emb)
    text_normed, text_len = unit_rows(text_emb)
    image_half = image_normed.astype(jnp.bfloat16)
    text_half = text_normed.astype(jnp.bfloat16)
    columns = lax.broadcasted_iota(jnp.int32, (row_count, row_count), 1)
    own_labels = jnp.where(positives[0][:, None] == columns, 1.0, -1.0).astype(jnp.float32)
    apart_labels = -jnp.ones((row_count, row_count), jnp.float32)
    own_flags = lax.dynamic_index_in_dim(pair_mask, myself, 0, keepdims=False)
    fetched = {}
    for direction in (1, -1):
        moving = text_half
        for distance in range(1, reach + 1):
            moving = passed_along(moving, BLK, -direction)
            fetched[direction * distance] = moving
    slopes, loss_sum = masked_tile(
        own_flags[reach], image_half, text_half, own_labels, logit_scale, offset
    )
    image_total = jnp.dot(slopes, text_half, preferred_element_type=jnp.float32)
    text_total = jnp.einsum("rc,rd->cd", slopes, image_half, preferred_element_type=jnp.float32)
    for distance in range(-reach, reach + 1):
        if distance == 0:
            continue
        partner = fetched[distance]
        slopes, part_loss = masked_tile(
            own_flags[reach + distance], image_half, partner, apart_labels, logit_scale, offset
        )
        loss_sum = loss_sum + part_loss
        image_total = image_total + jnp.dot(slopes, partner, preferred_element_type=jnp.float32)
        partial_grad = jnp.einsum(
            "rc,rd->cd", slopes, image_half, preferred_element_type=jnp.float32
        ).astype(jnp.bfloat16)
        arrived = passed_along(partial_grad, BLK, distance)
        text_total = text_total + arrived.astype(jnp.float32)
    total_loss = by_axis(loss_sum, BLK_GRP)
    image_count = row_count * block_count * lax.axis_size(GRP)
    loss = (total_loss / image_count).reshape(1)
    image_grad = back_rows(image_normed, image_len, image_total).astype(jnp.bfloat16)
    text_grad = back_rows(text_normed, text_len, text_total).astype(jnp.bfloat16)
    return (image_grad, text_grad, loss)


def solution(mesh):
    finer = Mesh(
        mesh.devices.reshape(2, 4, 16, 2, 2), ("blk_0", "blk_1", "blk_2", "grp_0", "grp_1")
    )
    in_specs = (P(BLK_GRP, None), P(BLK_GRP, None), P(BLK_GRP, None), P(), P(), P())
    out_specs = (P(BLK_GRP, None), P(BLK_GRP, None), P())
    return jax.shard_map(body, mesh=finer, in_specs=in_specs, out_specs=out_specs, check_vma=False)
```

profile of v0, /device:TPU:2, one launch (start us, length us, event | category | flops | bytes accessed | tf_op | source)
XLA Modules:
  0.0 277.3 jit_solution(6693817248874406426)
XLA Ops:
  0.7 1.5 fusion.27
  2.2 2.4 fusion.29
  4.5 15.5 %collective-permute-start.3 = (bf16[384,1152]{1,0:T(8,128)(2,1)}, bf16[384,1152]{1,0:T(8,128)(2,1)}, u32[]{:S(2)}, u32[]{:S(2)}) collective-permute-start(bf16[384,1152]{1,0:T(8,128)(2,1)} %fusion.29), channel_id=1, source_target_pairs={{0,508},{4,0},{8,4},{12,8},{16,12},{20,16},{24,20},{28,24},{32,28}... | collective-permute-start | bytes 2654216 | tf_op jit(solution)/shard_map/ppermute | solution.py:20
  20.1 1.9 collective-permute-start
  24.6 4.3 %conditional.7 = (bf16[384,384]{1,0:T(8,128)(2,1)S(1)}, f32[]{:T(128)}) conditional(s32[]{:T(128)} %bitcast, () %tuple.71, (s32[1,384]{1,0:T(1,128)S(1)}, s32[384,384]{1,0:T(8,128)S(1)}, f32[]{:T(128)}, bf16[384,1152]{1,0:T(8,128)(2,1)S(1)}, bf16[384,1152]{1,0:T(8,128)(2,1)}, /*index=5*/f32[]{:T(128)}) %tuple.115), branch_computations={%region_2.3_spmd, %region_3.5_spmd} | conditional | flops 342540288 | bytes 2658848 | solution.py:58
  24.7 3.6 %fusion.23 = (f32[]{:T(128)}, bf16[384,384]{1,0:T(8,128)(2,1)S(1)}) fusion(f32[]{:T(128)} %get-tuple-element.82, f32[]{:T(128)} %get-tuple-element.85, bf16[384,1152]{1,0:T(8,128)(2,1)S(1)} %get-tuple-element.83, bf16[384,1152]{1,0:T(8,128)(2,1)} %get-tuple-element.84, s32[384,384]{1,0:T(8,128)S(1)} %get-tuple-element.81, s32[384]{0:T(512)S(1)} %reduce), kind=kOutput, calls=%fused_computation.44 | convolution fusion | flops 342540288 | bytes 2655756 | tf_op jit(solution)/shard_map/cond/branch_1_fun/rd,cd->rc/dot_general | solution.py:39
  29.0 20.1 %collective-permute-done = bf16[384,1152]{1,0:T(8,128)(2,1)} collective-permute-done((bf16[384,1152]{1,0:T(8,128)(2,1)}, bf16[384,1152]{1,0:T(8,128)(2,1)}, u32[]{:S(2)}, u32[]{:S(2)}) %collective-permute-start) | collective-permute-done | bytes 884768 | tf_op jit(solution)/shard_map/ppermute | solution.py:20
  49.1 1.9 collective-permute-start.1
  51.0 9.6 %collective-permute-start.4 = (bf16[384,1152]{1,0:T(8,128)(2,1)}, bf16[384,1152]{1,0:T(8,128)(2,1)}, u32[]{:S(2)}, u32[]{:S(2)}) collective-permute-start(bf16[384,1152]{1,0:T(8,128)(2,1)} %collective-permute-done.3), channel_id=1, source_target_pairs={{0,508},{4,0},{8,4},{12,8},{16,12},{20,16},{24,20},{28,24},{32,28}... | collective-permute-start | bytes 2654216 | tf_op jit(solution)/shard_map/ppermute | solution.py:20
  60.7 1.9 fusion.31
  66.4 1.9 fusion.34
  69.1 1.6 convolution_convert_fusion.2
  70.7 1.9 collective-permute-start.9
  72.6 0.7 conditional.10
  73.3 2.6 convolution_convert_fusion.3
  75.9 13.7 %collective-permute-start.8 = (bf16[384,1152]{1,0:T(8,128)(2,1)}, bf16[384,1152]{1,0:T(8,128)(2,1)}, u32[]{:S(2)}, u32[]{:S(2)}) collective-permute-start(bf16[384,1152]{1,0:T(8,128)(2,1)} %convolution_convert_fusion.3), channel_id=1, source_target_pairs={{0,508},{4,0},{8,4},{12,8},{16,12},{20,16},{24,20},{28,24},{32,28}... | collective-permute-start | bytes 2654216 | tf_op jit(solution)/shard_map/ppermute | solution.py:20
  89.6 1.9 collective-permute-start.2
  91.6 9.6 %collective-permute-start.5 = (bf16[384,1152]{1,0:T(8,128)(2,1)}, bf16[384,1152]{1,0:T(8,128)(2,1)}, u32[]{:S(2)}, u32[]{:S(2)}) collective-permute-start(bf16[384,1152]{1,0:T(8,128)(2,1)} %collective-permute-done.4), channel_id=1, source_target_pairs={{0,508},{4,0},{8,4},{12,8},{16,12},{20,16},{24,20},{28,24},{32,28}... | collective-permute-start | bytes 2654216 | tf_op jit(solution)/shard_map/ppermute | solution.py:20
  101.2 3.0 %fusion.33 = f32[384,1152]{1,0:T(8,128)} fusion(bf16[384,384]{1,0:T(8,128)(2,1)S(1)} %copy-done.8, bf16[384,1152]{1,0:T(8,128)(2,1)} %collective-permute-done.3), kind=kOutput, calls=%fused_computation.77 | convolution fusion | flops 339738624 | bytes 2949120 | tf_op jit(solution)/shard_map/dot_general | solution.py:95
  104.2 3.1 %fusion.32 = f32[384,1152]{1,0:T(8,128)} fusion(bf16[384,384]{1,0:T(8,128)(2,1)} %get-tuple-element.130, bf16[384,1152]{1,0:T(8,128)(2,1)} %collective-permute-done), kind=kOutput, calls=%fused_computation.76 | convolution fusion | flops 339738624 | bytes 2949120 | tf_op jit(solution)/shard_map/dot_general | solution.py:95
  108.1 1.6 convolution_convert_fusion.1
  109.7 1.9 collective-permute-start.10
  111.7 0.8 conditional.9
  111.7 0.8 broadcast.45
  112.4 2.6 convolution_convert_fusion.4
  115.0 16.3 %collective-permute-done.2 = bf16[384,1152]{1,0:T(8,128)(2,1)} collective-permute-done((bf16[384,1152]{1,0:T(8,128)(2,1)}, bf16[384,1152]{1,0:T(8,128)(2,1)}, u32[]{:S(2)}, u32[]{:S(2)}) %collective-permute-start.2) | collective-permute-done | bytes 884768 | tf_op jit(solution)/shard_map/ppermute | solution.py:20
  131.3 0.7 conditional.8
  132.1 4.8 %conditional.13 = (bf16[384,384]{1,0:T(8,128)(2,1)}, f32[]{:T(128)}) conditional(s32[]{:T(128)} %bitcast.8, () %tuple.83, (f32[]{:T(128)}, bf16[384,1152]{1,0:T(8,128)(2,1)S(1)}, bf16[384,1152]{1,0:T(8,128)(2,1)}, f32[]{:T(128)}) %tuple.84), branch_computations={%region_20.21_spmd, %region_21.23_spmd} | conditional | flops 341950464 | bytes 2064412 | solution.py:58
  132.1 4.2 %fusion.17 = (f32[]{:T(128)}, bf16[384,384]{1,0:T(8,128)(2,1)}) fusion(f32[]{:T(128)} %get-tuple-element.106, f32[]{:T(128)} %get-tuple-element.109, bf16[384,1152]{1,0:T(8,128)(2,1)S(1)} %get-tuple-element.107, bf16[384,1152]{1,0:T(8,128)(2,1)} %get-tuple-element.108), kind=kOutput, calls=%fused_computation.34 | convolution fusion | flops 341950464 | bytes 2064396 | tf_op jit(solution)/shard_map/cond/branch_1_fun/rd,cd->rc/dot_general | solution.py:39
  136.9 7.5 %collective-permute-start.7 = (bf16[384,1152]{1,0:T(8,128)(2,1)}, bf16[384,1152]{1,0:T(8,128)(2,1)}, u32[]{:S(2)}, u32[]{:S(2)}) collective-permute-start(bf16[384,1152]{1,0:T(8,128)(2,1)} %convolution_convert_fusion.4), channel_id=1, source_target_pairs={{0,504},{4,508},{8,0},{12,4},{16,8},{20,12},{24,16},{28,20},{32,24... | collective-permute-start | bytes 2654216 | tf_op jit(solution)/shard_map/ppermute | solution.py:20
  144.4 6.9 %psum.35 = f32[]{:T(128)} all-reduce(f32[]{:T(128)S(6)} %add.201), channel_id=1, replica_groups=mesh['blk_0'=2,'blk_1'=4,'blk_2'=16,'grp_0'=2,'grp_1'=2] {'blk_0'}, use_global_device_ids=true, to_apply=%region_25.26 | all-reduce | flops 1 | bytes 8 | tf_op jit(solution)/shard_map/psum | solution.py:24
  151.3 2.6 convolution_convert_fusion.5
  153.9 8.3 %psum.36 = f32[]{:T(128)} all-reduce(f32[]{:T(128)} %psum.35), channel_id=1, replica_groups=mesh['blk_0'=2,'blk_1'=4,'blk_2'=16,'grp_0'=2,'grp_1'=2] {'blk_1'}, use_global_device_ids=true, to_apply=%region_26.27 | all-reduce | flops 1 | bytes 8 | tf_op jit(solution)/shard_map/psum | solution.py:24
  162.2 3.2 %convolution_add_fusion.3 = f32[384,1152]{1,0:T(8,128)} fusion(f32[384,1152]{1,0:T(8,128)S(1)} %fusion.31, bf16[384,384]{1,0:T(8,128)(2,1)} %get-tuple-element.128, bf16[384,1152]{1,0:T(8,128)(2,1)} %collective-permute-done.2), kind=kOutput, calls=%fused_computation.51 | convolution fusion | flops 340180992 | bytes 4718592 | tf_op jit(solution)/shard_map/dot_general | solution.py:95
  165.4 2.7 convolution_convert_fusion
  168.1 39.3 %psum.37 = f32[]{:T(128)} all-reduce(f32[]{:T(128)} %psum.36), channel_id=1, replica_groups=mesh['blk_0'=2,'blk_1'=4,'blk_2'=16,'grp_0'=2,'grp_1'=2] {'blk_2'}, use_global_device_ids=true, to_apply=%region_27.28 | all-reduce | flops 1 | bytes 8 | tf_op jit(solution)/shard_map/psum | solution.py:24
  207.3 1.9 collective-permute-start.11
  209.3 5.6 %psum.38 = f32[]{:T(128)} all-reduce(f32[]{:T(128)} %psum.37), channel_id=1, replica_groups=mesh['blk_0'=2,'blk_1'=4,'blk_2'=16,'grp_0'=2,'grp_1'=2] {'grp_0'}, use_global_device_ids=true, to_apply=%region_28.29 | all-reduce | flops 1 | bytes 8 | tf_op jit(solution)/shard_map/psum | solution.py:24
  214.9 3.2 %fusion.25 = f32[384,1152]{1,0:T(8,128)S(1)} fusion(f32[384,1152]{1,0:T(8,128)} %fusion.33, f32[384,1152]{1,0:T(8,128)} %fusion.32, f32[384,1152]{1,0:T(8,128)S(1)} %copy-done.3, bf16[384,384]{1,0:T(8,128)(2,1)} %get-tuple-element.129, bf16[384,1152]{1,0:T(8,128)(2,1)} %collective-permute-done.1), kind=kOutput, calls=%fused_computation.50 | convolution fusion | flops 341065728 | bytes 8257536 | tf_op jit(solution)/shard_map/dot_general | solution.py:95
  218.0 1.8 convolution_add_fusion.1
  219.8 11.4 %collective-permute-start.6 = (bf16[384,1152]{1,0:T(8,128)(2,1)}, bf16[384,1152]{1,0:T(8,128)(2,1)S(1)}, u32[]{:S(2)}, u32[]{:S(2)}) collective-permute-start(bf16[384,1152]{1,0:T(8,128)(2,1)} %convolution_convert_fusion.5), channel_id=1, source_target_pairs={{0,500},{4,504},{8,508},{12,0},{16,4},{20,8},{24,12},{28,16},{32,2... | collective-permute-start | bytes 2654216 | tf_op jit(solution)/shard_map/ppermute | solution.py:20
  231.3 2.1 multiply_reduce_fusion.1
  233.4 3.1 %psum.39 = f32[]{:T(128)} all-reduce(f32[]{:T(128)} %psum.38), channel_id=1, replica_groups=mesh['blk_0'=2,'blk_1'=4,'blk_2'=16,'grp_0'=2,'grp_1'=2] {'grp_1'}, use_global_device_ids=true, to_apply=%region_29.30 | all-reduce | flops 1 | bytes 8 | tf_op jit(solution)/shard_map/psum | solution.py:24
  237.2 1.3 divide_convert_fusion.1
  238.5 13.9 %collective-permute-done.11 = bf16[384,1152]{1,0:T(8,128)(2,1)} collective-permute-done((bf16[384,1152]{1,0:T(8,128)(2,1)}, bf16[384,1152]{1,0:T(8,128)(2,1)}, u32[]{:S(2)}, u32[]{:S(2)}) %collective-permute-start.11) | collective-permute-done | bytes 884768 | tf_op jit(solution)/shard_map/ppermute | solution.py:20
  252.4 19.2 %collective-permute-done.6 = bf16[384,1152]{1,0:T(8,128)(2,1)S(1)} collective-permute-done((bf16[384,1152]{1,0:T(8,128)(2,1)}, bf16[384,1152]{1,0:T(8,128)(2,1)S(1)}, u32[]{:S(2)}, u32[]{:S(2)}) %collective-permute-start.6) | collective-permute-done | bytes 884768 | tf_op jit(solution)/shard_map/ppermute | solution.py:20
  271.6 3.3 %multiply_reduce_fusion = (f32[384]{0:T(512)S(1)}, f32[384,1152]{1,0:T(8,128)S(1)}) fusion(f32[384]{0:T(512)S(1)} %add_sqrt_fusion, bf16[384,1152]{1,0:T(8,128)(2,1)S(1)} %copy-done.1, bf16[384,1152]{1,0:T(8,128)(2,1)} %collective-permute-done.11, bf16[384,1152]{1,0:T(8,128)(2,1)} %collective-permute-done.10, bf16[384,1152]{1,0:T(8,128)(2,1)} %collective-permute-done.9, ...), kind=kLoop, calls=%fused_computation.65 | loop fusion | flops 7077504 | bytes 9735168 | tf_op jit(solution)/shard_map/reduce_sum | solution.py:34
  274.9 1.3 divide_convert_fusion
  (46 shorter events, 4.4 us)
Async XLA Ops:
  0.6 21.4 %copy-start = (s32[128,7]{0,1:T(8,128)S(1)}, s32[128,7]{0,1:T(8,128)}, u32[]{:S(2)}) copy-start(s32[128,7]{0,1:T(8,128)} %param.23) | copy-start | bytes 10756
  0.6 23.4 %copy-start.2 = (bf16[384,1152]{1,0:T(8,128)(2,1)S(1)}, bf16[384,1152]{1,0:T(8,128)(2,1)}, u32[]{:S(2)}) copy-start(bf16[384,1152]{1,0:T(8,128)(2,1)} %param.20) | copy-start | bytes 2654212
  4.5 20.1 %copy-start.11 = (s32[1,384]{1,0:T(1,128)S(1)}, s32[1,384]{1,0:T(1,128)}, u32[]{:S(2)}) copy-start(s32[1,384]{1,0:T(1,128)} %param.22) | copy-start | bytes 4612
  4.5 46.5 %collective-permute-start.3 = (bf16[384,1152]{1,0:T(8,128)(2,1)}, bf16[384,1152]{1,0:T(8,128)(2,1)}, u32[]{:S(2)}, u32[]{:S(2)}) collective-permute-start(bf16[384,1152]{1,0:T(8,128)(2,1)} %fusion.29), channel_id=1, source_target_pairs={{0,508},{4,0},{8,4},{12,8},{16,12},{20,16},{24,20},{28,24},{32,28}... | collective-permute-start | bytes 2654216 | tf_op jit(solution)/shard_map/ppermute | solution.py:20
  20.1 29.0 %collective-permute-start = (bf16[384,1152]{1,0:T(8,128)(2,1)}, bf16[384,1152]{1,0:T(8,128)(2,1)}, u32[]{:S(2)}, u32[]{:S(2)}) collective-permute-start(bf16[384,1152]{1,0:T(8,128)(2,1)} %fusion.29), channel_id=1, source_target_pairs={{0,4},{4,8},{8,12},{12,16},{16,20},{20,24},{24,28},{28,32},{32,36}... | collective-permute-start | bytes 2654216 | tf_op jit(solution)/shard_map/ppermute | solution.py:20
  29.0 31.7 %copy-start.5 = (bf16[384,384]{1,0:T(8,128)(2,1)}, bf16[384,384]{1,0:T(8,128)(2,1)S(1)}, u32[]{:S(2)}) copy-start(bf16[384,384]{1,0:T(8,128)(2,1)S(1)} %get-tuple-element.127) | copy-start | bytes 884740
  49.1 40.5 %collective-permute-start.1 = (bf16[384,1152]{1,0:T(8,128)(2,1)}, bf16[384,1152]{1,0:T(8,128)(2,1)}, u32[]{:S(2)}, u32[]{:S(2)}) collective-permute-start(bf16[384,1152]{1,0:T(8,128)(2,1)} %collective-permute-done), channel_id=1, source_target_pairs={{0,4},{4,8},{8,12},{12,16},{16,20},{20,24},{24,28},{28,32},{32,36}... | collective-permute-start | bytes 2654216 | tf_op jit(solution)/shard_map/ppermute | solution.py:20
  51.0 40.5 %collective-permute-start.4 = (bf16[384,1152]{1,0:T(8,128)(2,1)}, bf16[384,1152]{1,0:T(8,128)(2,1)}, u32[]{:S(2)}, u32[]{:S(2)}) collective-permute-start(bf16[384,1152]{1,0:T(8,128)(2,1)} %collective-permute-done.3), channel_id=1, source_target_pairs={{0,508},{4,0},{8,4},{12,8},{16,12},{20,16},{24,20},{28,24},{32,28}... | collective-permute-start | bytes 2654216 | tf_op jit(solution)/shard_map/ppermute | solution.py:20
  60.7 5.7 %copy-start.6 = (bf16[384,384]{1,0:T(8,128)(2,1)S(1)}, bf16[384,384]{1,0:T(8,128)(2,1)}, u32[]{:S(2)}) copy-start(bf16[384,384]{1,0:T(8,128)(2,1)} %copy-done.5) | copy-start | bytes 884740
  68.4 0.7 copy-start.7
  70.7 149.2 %collective-permute-start.9 = (bf16[384,1152]{1,0:T(8,128)(2,1)}, bf16[384,1152]{1,0:T(8,128)(2,1)}, u32[]{:S(2)}, u32[]{:S(2)}) collective-permute-start(bf16[384,1152]{1,0:T(8,128)(2,1)} %convolution_convert_fusion.2), channel_id=1, source_target_pairs={{0,4},{4,8},{8,12},{12,16},{16,20},{20,24},{24,28},{28,32},{32,36}... | collective-permute-start | bytes 2654216 | tf_op jit(solution)/shard_map/ppermute | solution.py:20
  73.3 27.9 %copy-start.8 = (bf16[384,384]{1,0:T(8,128)(2,1)S(1)}, bf16[384,384]{1,0:T(8,128)(2,1)}, u32[]{:S(2)}) copy-start(bf16[384,384]{1,0:T(8,128)(2,1)} %copy-done.7) | copy-start | bytes 884740
  75.9 162.5 %collective-permute-start.8 = (bf16[384,1152]{1,0:T(8,128)(2,1)}, bf16[384,1152]{1,0:T(8,128)(2,1)}, u32[]{:S(2)}, u32[]{:S(2)}) collective-permute-start(bf16[384,1152]{1,0:T(8,128)(2,1)} %convolution_convert_fusion.3), channel_id=1, source_target_pairs={{0,508},{4,0},{8,4},{12,8},{16,12},{20,16},{24,20},{28,24},{32,28}... | collective-permute-start | bytes 2654216 | tf_op jit(solution)/shard_map/ppermute | solution.py:20
  89.6 41.7 %collective-permute-start.2 = (bf16[384,1152]{1,0:T(8,128)(2,1)}, bf16[384,1152]{1,0:T(8,128)(2,1)}, u32[]{:S(2)}, u32[]{:S(2)}) collective-permute-start(bf16[384,1152]{1,0:T(8,128)(2,1)} %collective-permute-done.1), channel_id=1, source_target_pairs={{0,4},{4,8},{8,12},{12,16},{16,20},{20,24},{24,28},{28,32},{32,36}... | collective-permute-start | bytes 2654216 | tf_op jit(solution)/shard_map/ppermute | solution.py:20
  91.6 40.5 %collective-permute-start.5 = (bf16[384,1152]{1,0:T(8,128)(2,1)}, bf16[384,1152]{1,0:T(8,128)(2,1)}, u32[]{:S(2)}, u32[]{:S(2)}) collective-permute-start(bf16[384,1152]{1,0:T(8,128)(2,1)} %collective-permute-done.4), channel_id=1, source_target_pairs={{0,508},{4,0},{8,4},{12,8},{16,12},{20,16},{24,20},{28,24},{32,28}... | collective-permute-start | bytes 2654216 | tf_op jit(solution)/shard_map/ppermute | solution.py:20
  107.4 0.7 copy-start.9
  109.7 128.8 %collective-permute-start.10 = (bf16[384,1152]{1,0:T(8,128)(2,1)}, bf16[384,1152]{1,0:T(8,128)(2,1)}, u32[]{:S(2)}, u32[]{:S(2)}) collective-permute-start(bf16[384,1152]{1,0:T(8,128)(2,1)} %convolution_convert_fusion.1), channel_id=1, source_target_pairs={{0,8},{4,12},{8,16},{12,20},{16,24},{20,28},{24,32},{28,36},{32,40... | collective-permute-start | bytes 2654216 | tf_op jit(solution)/shard_map/ppermute | solution.py:20
  136.9 101.6 %collective-permute-start.7 = (bf16[384,1152]{1,0:T(8,128)(2,1)}, bf16[384,1152]{1,0:T(8,128)(2,1)}, u32[]{:S(2)}, u32[]{:S(2)}) collective-permute-start(bf16[384,1152]{1,0:T(8,128)(2,1)} %convolution_convert_fusion.4), channel_id=1, source_target_pairs={{0,504},{4,508},{8,0},{12,4},{16,8},{20,12},{24,16},{28,20},{32,24... | collective-permute-start | bytes 2654216 | tf_op jit(solution)/shard_map/ppermute | solution.py:20
  165.4 49.4 %copy-start.3 = (f32[384,1152]{1,0:T(8,128)S(1)}, f32[384,1152]{1,0:T(8,128)}, u32[]{:S(2)}) copy-start(f32[384,1152]{1,0:T(8,128)} %convolution_add_fusion.3) | copy-start | bytes 5308420
  207.3 45.1 %collective-permute-start.11 = (bf16[384,1152]{1,0:T(8,128)(2,1)}, bf16[384,1152]{1,0:T(8,128)(2,1)}, u32[]{:S(2)}, u32[]{:S(2)}) collective-permute-start(bf16[384,1152]{1,0:T(8,128)(2,1)} %convolution_convert_fusion), channel_id=1, source_target_pairs={{0,12},{4,16},{8,20},{12,24},{16,28},{20,32},{24,36},{28,40},{32,4... | collective-permute-start | bytes 2654216 | tf_op jit(solution)/shard_map/ppermute | solution.py:20
  214.9 3.2 %copy-start.10 = (bf16[384,384]{1,0:T(8,128)(2,1)S(1)}, bf16[384,384]{1,0:T(8,128)(2,1)}, u32[]{:S(2)}) copy-start(bf16[384,384]{1,0:T(8,128)(2,1)} %copy-done.9) | copy-start | bytes 884740
  219.8 51.8 %collective-permute-start.6 = (bf16[384,1152]{1,0:T(8,128)(2,1)}, bf16[384,1152]{1,0:T(8,128)(2,1)S(1)}, u32[]{:S(2)}, u32[]{:S(2)}) collective-permute-start(bf16[384,1152]{1,0:T(8,128)(2,1)} %convolution_convert_fusion.5), channel_id=1, source_target_pairs={{0,500},{4,504},{8,508},{12,0},{16,4},{20,8},{24,12},{28,16},{32,2... | collective-permute-start | bytes 2654216 | tf_op jit(solution)/shard_map/ppermute | solution.py:20
  237.2 34.5 %copy-start.1 = (bf16[384,1152]{1,0:T(8,128)(2,1)S(1)}, bf16[384,1152]{1,0:T(8,128)(2,1)}, u32[]{:S(2)}) copy-start(bf16[384,1152]{1,0:T(8,128)(2,1)} %param.21) | copy-start | bytes 2654212
  237.2 34.4 %copy-start.4 = (f32[384,1152]{1,0:T(8,128)S(1)}, f32[384,1152]{1,0:T(8,128)}, u32[]{:S(2)}) copy-start(f32[384,1152]{1,0:T(8,128)} %fusion.34) | copy-start | bytes 5308420
where the time goes:
time: 279 us; the launch traced here: 277 us
  starting transfers between devices  78.9 us (28%)
  waiting for transfers between devices  69.6 us (25%)
  blocking collectives  63.2 us (23%)
  matrix products  41.6 us (15%)
  other arithmetic  10.3 us (4%)
  between operations  7.87 us (3%)
  local copies, waits for them, and re-layouts  4.46 us (2%)
    ppermute x12, starting transfers between devices, passed_along(): return lax.ppermute(value, axis, pairs)  78.9 us
    ppermute x12, waiting for transfers between devices, passed_along(): return lax.ppermute(value, axis, pairs)  69.6 us
    psum x5, blocking collectives, by_axis(): return functools.reduce(lax.psum, axes, shard)  63.2 us
    dot_general x6, matrix products, body(): jnp.dot(slopes, partner, preferred_element_type=jnp.float32)  16.4 us
    dot_general x7, matrix products, body(): jnp.einsum('rc,rd->cd', slopes, image_half, preferred_element_type=jnp.fl...  15.5 us
    dot_general x2, matrix products, score_tile(): jnp.einsum('rd,cd->rc', image_side, text_side, preferred_element_type=jnp...  7.81 us
  transfers between devices with their start and end apart: 12, of which 4 were waited for; matrix products, arithmetic and copies ran while one was open for 17% of the time, Pallas kernels for 0%

commit v1 on v0

v1 whole, which is shorter than its diff:
```python
import functools

import jax
import jax.numpy as jnp
from jax import lax
from jax.experimental import pallas as pl
from jax.experimental.pallas import tpu as pltpu
from jax.sharding import Mesh
from jax.sharding import PartitionSpec as P

ALL = ("x_hi", "y", "z", "x_lo", "core")
BLK = ("x_hi", "y", "z")

EPSILON = 1e-06
VMEM_LIMIT = 32 * 1024 * 1024


def shifted(value, axis, steps):
    count = lax.axis_size(axis)
    return lax.ppermute(value, axis, [(s, (s + steps) % count) for s in range(count)])


def dot(a, b, contract):
    return lax.dot_general(a, b, ((contract[:1], contract[1:]), ((), ())), preferred_element_type=jnp.float32)


def unit_of(raw):
    values = raw.astype(jnp.float32)
    inverse = lax.rsqrt(jnp.sum(values * values, axis=1, keepdims=True) + EPSILON)
    return values * inverse, inverse


def loss_and_sigmoid(u):
    small = jnp.exp(-jnp.abs(u))
    loss = jnp.maximum(u, 0.0) + jnp.log1p(small)
    return loss, jnp.where(u >= 0.0, 1.0, small) / (1.0 + small)


def own_kernel(scal, positives, image, text, image_half, text_half, image_acc, text_acc, loss):
    image_half[...] = unit_of(image[...])[0].astype(jnp.bfloat16)
    text_half[...] = unit_of(text[...])[0].astype(jnp.bfloat16)
    z = scal[0] * dot(text_half[...], image_half[...], (1, 1)) + scal[1]
    match = lax.broadcasted_iota(jnp.int32, z.shape, 0) == positives[...]
    part, sigmoid = loss_and_sigmoid(jnp.where(match, -z, z))
    loss[0] = jnp.sum(part)
    slopes = (jnp.where(match, -sigmoid, sigmoid) * scal[0]).astype(jnp.bfloat16)
    text_acc[...] = dot(slopes, image_half[...], (1, 0))
    image_acc[...] = dot(slopes, text_half[...], (0, 0))


def pair_kernel(which, with_loss, last, flags, scal, *refs):
    refs = list(refs)
    loss_in = refs.pop(0) if with_loss else None
    half, acc = refs.pop(0), refs.pop(0)
    raw = refs.pop(0) if last else None
    partners = [refs.pop(0) for _ in which]
    out = refs.pop(0)
    loss_out = refs.pop(0) if with_loss else None
    total = refs.pop(0) if last else out
    total[...] = acc[...]
    if with_loss:
        loss_out[0] = loss_in[0]
    for (row, column), partner in zip(which, partners):

        @pl.when(flags[row, column] > 0)
        def _(partner=partner):
            other = unit_of(partner[...])[0].astype(jnp.bfloat16)
            z = scal[0] * dot(half[...], other, (1, 1)) + scal[1]
            part, sigmoid = loss_and_sigmoid(z)
            if with_loss:
                loss_out[0] = loss_out[0] + jnp.sum(part)
            slopes = (sigmoid * scal[0]).astype(jnp.bfloat16)
            total[...] += dot(slopes, other, (1, 0))

    if last:
        unit, inverse = unit_of(raw[...])
        upstream = total[...]
        inward = jnp.sum(unit * upstream, axis=1, keepdims=True)
        out[...] = ((upstream - unit * inward) * inverse).astype(jnp.bfloat16)


SMEM = pl.BlockSpec(memory_space=pltpu.SMEM)
VMEM = pl.BlockSpec(memory_space=pltpu.VMEM)


def cost(pairs, blocks):
    return pl.CostEstimate(flops=pairs * 4 * 384 * 384 * 1152, bytes_accessed=blocks * 384 * 1152 * 2, transcendentals=pairs * 3 * 384 * 384)


def own_pair(scal, positives, image, text):
    shape = image.shape
    return pl.pallas_call(
        own_kernel,
        out_shape=[jax.ShapeDtypeStruct(shape, jnp.bfloat16)] * 2 + [jax.ShapeDtypeStruct(shape, jnp.float32)] * 2 + [jax.ShapeDtypeStruct((1,), jnp.float32)],
        in_specs=[SMEM, VMEM, VMEM, VMEM],
        out_specs=[VMEM] * 4 + [SMEM],
        compiler_params=pltpu.CompilerParams(vmem_limit_bytes=VMEM_LIMIT),
        cost_estimate=cost(2, 8),
        name="own_pair",
    )(scal, positives, image, text)


def add_pairs(which, flags, scal, loss, half, acc, raw, partners, name):
    with_loss, last = loss is not None, raw is not None
    operands = [flags, scal] + ([loss] if with_loss else []) + [half, acc] + ([raw] if last else []) + list(partners)
    in_specs = [SMEM, SMEM] + ([SMEM] if with_loss else []) + [VMEM] * (2 + last + len(partners))
    out_shape = [jax.ShapeDtypeStruct(acc.shape, jnp.bfloat16 if last else jnp.float32)]
    out_specs = [VMEM]
    if with_loss:
        out_shape.append(jax.ShapeDtypeStruct((1,), jnp.float32))
        out_specs.append(SMEM)
    aliases = {} if last else {3 + with_loss: 0}
    return pl.pallas_call(
        functools.partial(pair_kernel, tuple(which), with_loss, last),
        out_shape=out_shape,
        in_specs=in_specs,
        out_specs=out_specs,
        scratch_shapes=[pltpu.VMEM(acc.shape, jnp.float32)] if last else [],
        input_output_aliases=aliases,
        compiler_params=pltpu.CompilerParams(vmem_limit_bytes=VMEM_LIMIT),
        cost_estimate=cost(len(partners), 6 + len(partners)),
        name=name,
    )(*operands)


def flags_of(pair_mask, reach):
    count = pair_mask.shape[0]
    me = lax.axis_index(BLK)
    block = lax.broadcasted_iota(jnp.int32, pair_mask.shape, 0)
    e = lax.broadcasted_iota(jnp.int32, pair_mask.shape, 1) - reach
    mine = jnp.sum(jnp.where(block == me, pair_mask, 0), axis=0)
    theirs = jnp.sum(jnp.where(block == lax.rem(me - e + count, count), pair_mask, 0), axis=0)
    return jnp.stack([mine, theirs])


def summed(value):
    for axis in ("core", "x_lo", "x_hi", "y", "z"):
        step = 1
        while step < lax.axis_size(axis):
            value = value + shifted(value, axis, step)
            step *= 2
    return value


def body(image_emb, text_emb, positives, pair_mask, log_scale, bias):
    reach = (pair_mask.shape[1] - 1) // 2
    scal = jnp.concatenate([jnp.exp(log_scale), bias])
    flags = flags_of(pair_mask, reach)

    texts, images = {0: text_emb}, {0: image_emb}
    for distance in range(1, reach + 1):
        for held in (texts, images):
            for sign in (1, -1):
                held[sign * distance] = shifted(held[sign * (distance - 1)], BLK, -sign)

    image_half, text_half, image_acc, text_acc, loss = own_pair(scal, positives, image_emb, text_emb)
    for d in range(1, reach + 1):
        last = d == reach
        image_acc, loss = add_pairs(
            [(0, reach + d), (0, reach - d)], flags, scal, loss, image_half, image_acc,
            image_emb if last else None, [texts[d], texts[-d]], f"image_side_{d}",
        )
        (text_acc,) = add_pairs(
            [(1, reach - d), (1, reach + d)], flags, scal, None, text_half, text_acc,
            text_emb if last else None, [images[d], images[-d]], f"text_side_{d}",
        )
    total = summed(loss)
    image_count = image_emb.shape[0] * lax.axis_size(ALL)
    return image_acc, text_acc, total / image_count


def solution(mesh):
    fine = Mesh(mesh.devices.reshape(2, 4, 16, 2, 2), ALL)
    rows = P(ALL, None)
    return jax.shard_map(
        body,
        mesh=fine,
        in_specs=(rows, rows, rows, P(), P(), P()),
        out_specs=(rows, rows, P()),
        check_vma=False,
    )
```

time: 279 us -> 215 us (0.77)
  blocking collectives: 63.2 us -> 0 us
  matrix products: 41.6 us -> 0 us
  starting transfers between devices: 78.9 us -> 107 us
  Pallas kernels: 0 us -> 19.4 us
  other arithmetic: 10.3 us -> 1.01 us
  waiting for transfers between devices: 69.6 us -> 73.8 us
    psum x5 -> x0, blocking collectives: 63.2 us -> none  [by_axis(): return functools.reduce(lax.psum, axes, shard)]
    dot_general x16 -> x0, matrix products: 41.6 us -> none  [the longest x6 16.4 us: body(): jnp.dot(slopes, partner, preferred_element_type=jnp.float32)]
    ppermute x12 -> x21, starting transfers between devices: 78.9 us -> 107 us  [shifted(): lax.ppermute(value, axis, [(s, (s + steps) % count) for s in range(count)])]
    pallas_call x0 -> x7, Pallas kernels: none -> 19.4 us  [the longest x6 16.2 us: add_pairs(): pl.pallas_call(functools.partial(pair_kernel, tuple(which), with_loss, la...]
    convert_element_type x4 -> x0, other arithmetic: 5.27 us -> none  [the longest x1 2.35 us: body(): text_half = text_normed.astype(jnp.bfloat16)]
    ppermute x12 -> x21, waiting for transfers between devices: 69.6 us -> 73.8 us  [shifted(): lax.ppermute(value, axis, [(s, (s + steps) % count) for s in range(count)])]
    reduce_sum x3 -> x1, other arithmetic: 5.03 us -> 0.9 us  [flags_of(): mine = jnp.sum(jnp.where(block == me, pair_mask, 0), axis=0)]
  transfers between devices with their start and end apart: 12 -> 21, of which waited for: 4 -> 19; matrix products, arithmetic and copies ran while one was open for 17% -> 0% of each run, Pallas kernels for 0% -> 9%
where the time goes in v1:
time: 215 us; the launch traced here: 214 us
  starting transfers between devices  107 us (50%)
  waiting for transfers between devices  73.8 us (34%)
  Pallas kernels  19.4 us (9%)
  between operations  9.18 us (4%)
  local copies, waits for them, and re-layouts  3.02 us (1%)
    ppermute x21, starting transfers between devices, shifted(): lax.ppermute(value, axis, [(s, (s + steps) % count) for s in range(count)])  107 us
    ppermute x21, waiting for transfers between devices, shifted(): lax.ppermute(value, axis, [(s, (s + steps) % count) for s in range(count)])  73.8 us
    pallas_call x6, Pallas kernels, add_pairs(): pl.pallas_call(functools.partial(pair_kernel, tuple(which), with_loss, la...  16.2 us
  transfers between devices with their start and end apart: 21, of which 19 were waited for; matrix products, arithmetic and copies ran while one was open for 0% of the time, Pallas kernels for 9%

profile of v1, /device:TPU:2, one launch (start us, length us, event | category | flops | bytes accessed | tf_op | source)
XLA Modules:
  0.0 213.6 jit_solution(15961610608117779593)
XLA Ops:
  0.6 15.4 %collective-permute-start = (bf16[384,1152]{1,0:T(8,128)(2,1)}, bf16[384,1152]{1,0:T(8,128)(2,1)}, u32[]{:S(2)}, u32[]{:S(2)}) collective-permute-start(bf16[384,1152]{1,0:T(8,128)(2,1)} %refs_2_.1), channel_id=1, source_target_pairs={{0,508},{4,0},{8,4},{12,8},{16,12},{20,16},{24,20},{28,24},{32,28}... | collective-permute-start | bytes 2654216 | tf_op jit(solution)/shard_map/ppermute | solution.py:20
  16.1 1.9 collective-permute-start.1
  18.0 9.6 %collective-permute-start.6 = (bf16[384,1152]{1,0:T(8,128)(2,1)}, bf16[384,1152]{1,0:T(8,128)(2,1)S(1)}, u32[]{:S(2)}, u32[]{:S(2)}) collective-permute-start(bf16[384,1152]{1,0:T(8,128)(2,1)} %refs_3_.1), channel_id=1, source_target_pairs={{0,508},{4,0},{8,4},{12,8},{16,12},{20,16},{24,20},{28,24},{32,28}... | collective-permute-start | bytes 2654216 | tf_op jit(solution)/shard_map/ppermute | solution.py:20
  27.6 1.9 collective-permute-start.7
  29.6 6.8 %collective-permute-done.refs_3_ = bf16[384,1152]{1,0:T(8,128)(2,1)} collective-permute-done((bf16[384,1152]{1,0:T(8,128)(2,1)}, bf16[384,1152]{1,0:T(8,128)(2,1)}, u32[]{:S(2)}, u32[]{:S(2)}) %collective-permute-start) | collective-permute-done | bytes 884768 | tf_op jit(solution)/shard_map/ppermute | solution.py:20
  36.4 10.1 %collective-permute-start.2 = (bf16[384,1152]{1,0:T(8,128)(2,1)}, bf16[384,1152]{1,0:T(8,128)(2,1)}, u32[]{:S(2)}, u32[]{:S(2)}) collective-permute-start(bf16[384,1152]{1,0:T(8,128)(2,1)} %collective-permute-done.refs_3_), channel_id=1, source_target_pairs={{0,508},{4,0},{8,4},{12,8},{16,12},{20,16},{24,20},{28,24},{32,28}... | collective-permute-start | bytes 2654216 | tf_op jit(solution)/shard_map/ppermute | solution.py:20
  46.6 1.9 collective-permute-start.3
  48.5 6.9 %collective-permute-done.6.refs_2_ = bf16[384,1152]{1,0:T(8,128)(2,1)S(1)} collective-permute-done((bf16[384,1152]{1,0:T(8,128)(2,1)}, bf16[384,1152]{1,0:T(8,128)(2,1)S(1)}, u32[]{:S(2)}, u32[]{:S(2)}) %collective-permute-start.6) | collective-permute-done | bytes 884768 | tf_op jit(solution)/shard_map/ppermute | solution.py:20
  55.4 10.0 %collective-permute-start.8 = (bf16[384,1152]{1,0:T(8,128)(2,1)S(1)}, bf16[384,1152]{1,0:T(8,128)(2,1)S(1)}, u32[]{:S(2)}, u32[]{:S(2)}) collective-permute-start(bf16[384,1152]{1,0:T(8,128)(2,1)S(1)} %collective-permute-done.6.refs_2_), channel_id=1, source_target_pairs={{0,508},{4,0},{8,4},{12,8},{16,12},{20,16},{24,20},{28,24},{32,28}... | collective-permute-start | bytes 2654216 | tf_op jit(solution)/shard_map/ppermute | solution.py:20
  65.4 1.9 collective-permute-start.9
  67.4 6.9 %collective-permute-done.2.refs_3_ = bf16[384,1152]{1,0:T(8,128)(2,1)} collective-permute-done((bf16[384,1152]{1,0:T(8,128)(2,1)}, bf16[384,1152]{1,0:T(8,128)(2,1)}, u32[]{:S(2)}, u32[]{:S(2)}) %collective-permute-start.2) | collective-permute-done | bytes 884768 | tf_op jit(solution)/shard_map/ppermute | solution.py:20
  74.3 10.1 %collective-permute-start.4 = (bf16[384,1152]{1,0:T(8,128)(2,1)}, bf16[384,1152]{1,0:T(8,128)(2,1)S(1)}, u32[]{:S(2)}, u32[]{:S(2)}) collective-permute-start(bf16[384,1152]{1,0:T(8,128)(2,1)} %collective-permute-done.2.refs_3_), channel_id=1, source_target_pairs={{0,508},{4,0},{8,4},{12,8},{16,12},{20,16},{24,20},{28,24},{32,28}... | collective-permute-start | bytes 2654216 | tf_op jit(solution)/shard_map/ppermute | solution.py:20
  84.5 1.9 collective-permute-start.5
  86.4 0.9 select_reduce_fusion.1
  88.7 4.5 %collective-permute-done.8.refs_2_ = bf16[384,1152]{1,0:T(8,128)(2,1)S(1)} collective-permute-done((bf16[384,1152]{1,0:T(8,128)(2,1)S(1)}, bf16[384,1152]{1,0:T(8,128)(2,1)S(1)}, u32[]{:S(2)}, u32[]{:S(2)}) %collective-permute-start.8) | collective-permute-done | bytes 884768 | tf_op jit(solution)/shard_map/ppermute | solution.py:20
  93.2 10.1 %collective-permute-start.10 = (bf16[384,1152]{1,0:T(8,128)(2,1)S(1)}, bf16[384,1152]{1,0:T(8,128)(2,1)S(1)}, u32[]{:S(2)}, u32[]{:S(2)}) collective-permute-start(bf16[384,1152]{1,0:T(8,128)(2,1)S(1)} %collective-permute-done.8.refs_2_), channel_id=1, source_target_pairs={{0,508},{4,0},{8,4},{12,8},{16,12},{20,16},{24,20},{28,24},{32,28}... | collective-permute-start | bytes 2654216 | tf_op jit(solution)/shard_map/ppermute | solution.py:20
  103.3 1.9 collective-permute-start.11
  105.3 0.1 pad_maximum_fusion.scal
  105.3 1.2 copy-done
  106.5 1.2 copy-done.2
  107.7 0.7 copy-done.4
  108.4 3.2 %own_pair.1 = (bf16[384,1152]{1,0:T(8,128)(2,1)S(1)}, bf16[384,1152]{1,0:T(8,128)(2,1)S(1)}, f32[384,1152]{1,0:T(8,128)S(1)}, f32[384,1152]{1,0:T(8,128)S(1)}, f32[1]{0:T(128)}) custom-call(f32[2]{0:T(128)S(1)} %pad_maximum_fusion.scal, s32[1,384]{1,0:T(1,128)S(1)} %copy-done.4, bf16[384,1152]{1,0:T(8,128)(2,1)S(1)} %copy-done, bf16[384,1152]{1,0:T(8,128)(2,1)S(1)} %copy-done.2), custom_call_target="tpu_custom_call" | custom-call | flops 1358954496 | bytes 7077888 | tf_op jit(solution)/shard_map/own_pair/pallas_call | solution.py:92
  111.6 0.8 text_side_1.1.refs_1_
  112.4 2.8 %image_side_1.1 = (f32[384,1152]{1,0:T(8,128)S(1)}, f32[1]{0:T(128)}) custom-call(s32[2,7]{1,0:T(2,128)S(1)} %pad_add_fusion.flags, f32[2]{0:T(128)S(1)} %pad_maximum_fusion.scal, f32[1]{0:T(128)} %get-tuple-element.14.refs_0_, bf16[384,1152]{1,0:T(8,128)(2,1)S(1)} %get-tuple-element.15.refs_1_, ...), custom_call_target="tpu_custom_call", output_to_operand_aliasing={{0}: (4, {})} | custom-call | flops 1358954496 | bytes 7077888 | tf_op jit(solution)/shard_map/image_side_1/pallas_call | solution.py:113
  115.2 2.6 %text_side_2.1.refs_1_ = f32[384,1152]{1,0:T(8,128)S(1)} custom-call(s32[2,7]{1,0:T(2,128)S(1)} %pad_add_fusion.flags, f32[2]{0:T(128)S(1)} %pad_maximum_fusion.scal, bf16[384,1152]{1,0:T(8,128)(2,1)S(1)} %get-tuple-element.22.refs_0_, f32[384,1152]{1,0:T(8,128)S(1)} %text_side_1.1.refs_1_, ...), custom_call_target="tpu_custom_call", output_to_operand_aliasing={{}: (3, {})} | custom-call | flops 1358954496 | bytes 7077888 | tf_op jit(solution)/shard_map/text_side_2/pallas_call | solution.py:113
  117.8 2.9 %image_side_2.1 = (f32[384,1152]{1,0:T(8,128)S(1)}, f32[1]{0:T(128)}) custom-call(s32[2,7]{1,0:T(2,128)S(1)} %pad_add_fusion.flags, f32[2]{0:T(128)S(1)} %pad_maximum_fusion.scal, f32[1]{0:T(128)} %get-tuple-element.17.refs_0_, bf16[384,1152]{1,0:T(8,128)(2,1)S(1)} %get-tuple-element.15.refs_1_, ...), custom_call_target="tpu_custom_call", output_to_operand_aliasing={{0}: (4, {})} | custom-call | flops 1358954496 | bytes 7077888 | tf_op jit(solution)/shard_map/image_side_2/pallas_call | solution.py:113
  120.8 1.5 collective-permute-done.5.refs_5_
  122.3 4.7 %image_side_3.1 = (bf16[384,1152]{1,0:T(8,128)(2,1)}, f32[1]{0:T(128)}) custom-call(s32[2,7]{1,0:T(2,128)S(1)} %pad_add_fusion.flags, f32[2]{0:T(128)S(1)} %pad_maximum_fusion.scal, f32[1]{0:T(128)} %get-tuple-element.19.refs_0_, bf16[384,1152]{1,0:T(8,128)(2,1)S(1)} %get-tuple-element.15.refs_1_, f32[384,1152]{1,0:T(8,128)S(1)} %get-tuple-element.20.refs_2_, ...), custom_call_target="tpu_custom_call" | custom-call | flops 1358954496 | bytes 7077888 | tf_op jit(solution)/shard_map/image_side_3/pallas_call | solution.py:113
  127.0 1.9 collective-permute-start.12
  129.0 1.0 collective-permute-done.10.refs_3_
  129.9 9.8 %collective-permute-done.11.refs_4_ = bf16[384,1152]{1,0:T(8,128)(2,1)S(1)} collective-permute-done((bf16[384,1152]{1,0:T(8,128)(2,1)S(1)}, bf16[384,1152]{1,0:T(8,128)(2,1)S(1)}, u32[]{:S(2)}, u32[]{:S(2)}) %collective-permute-start.11) | collective-permute-done | bytes 884768 | tf_op jit(solution)/shard_map/ppermute | solution.py:20
  139.8 2.4 %text_side_3.1 = bf16[384,1152]{1,0:T(8,128)(2,1)} custom-call(s32[2,7]{1,0:T(2,128)S(1)} %pad_add_fusion.flags, f32[2]{0:T(128)S(1)} %pad_maximum_fusion.scal, bf16[384,1152]{1,0:T(8,128)(2,1)S(1)} %get-tuple-element.22.refs_0_, f32[384,1152]{1,0:T(8,128)S(1)} %text_side_2.1.refs_1_, bf16[384,1152]{1,0:T(8,128)(2,1)S(1)} %copy-done.3, ...), custom_call_target="tpu_custom_call" | custom-call | flops 1358954496 | bytes 7077888 | tf_op jit(solution)/shard_map/text_side_3/pallas_call | solution.py:113
  143.4 4.6 %collective-permute-start.13 = (f32[1]{0:T(128)}, f32[1]{0:T(128)}, u32[]{:S(2)}, u32[]{:S(2)}) collective-permute-start(f32[1]{0:T(128)} %add.42), channel_id=1, source_target_pairs={{0,2},{2,0},{1,3},{3,1},{4,6},{6,4},{5,7},{7,5},{8,10},{10,8},{9,1... | collective-permute-start | bytes 20 | tf_op jit(solution)/shard_map/ppermute | solution.py:20
  148.1 0.9 collective-permute-done.13
  149.5 4.6 %collective-permute-start.14 = (f32[1]{0:T(128)}, f32[1]{0:T(128)}, u32[]{:S(2)}, u32[]{:S(2)}) collective-permute-start(f32[1]{0:T(128)} %add.43), channel_id=1, source_target_pairs={{0,256},{256,0},{1,257},{257,1},{2,258},{258,2},{3,259},{259,3},{4... | collective-permute-start | bytes 20 | tf_op jit(solution)/shard_map/ppermute | solution.py:20
  154.1 2.4 %collective-permute-done.14 = f32[1]{0:T(128)} collective-permute-done((f32[1]{0:T(128)}, f32[1]{0:T(128)}, u32[]{:S(2)}, u32[]{:S(2)}) %collective-permute-start.14) | collective-permute-done | bytes 36 | tf_op jit(solution)/shard_map/ppermute | solution.py:20
  157.2 3.2 %collective-permute-start.15 = (f32[1]{0:T(128)}, f32[1]{0:T(128)}, u32[]{:S(2)}, u32[]{:S(2)}) collective-permute-start(f32[1]{0:T(128)} %add.44), channel_id=1, source_target_pairs={{0,64},{64,128},{128,192},{192,0},{1,65},{65,129},{129,193},{193,1... | collective-permute-start | bytes 20 | tf_op jit(solution)/shard_map/ppermute | solution.py:20
  160.4 3.5 %collective-permute-done.15 = f32[1]{0:T(128)} collective-permute-done((f32[1]{0:T(128)}, f32[1]{0:T(128)}, u32[]{:S(2)}, u32[]{:S(2)}) %collective-permute-start.15) | collective-permute-done | bytes 36 | tf_op jit(solution)/shard_map/ppermute | solution.py:20
  164.5 3.2 %collective-permute-start.16 = (f32[1]{0:T(128)}, f32[1]{0:T(128)}, u32[]{:S(2)}, u32[]{:S(2)}) collective-permute-start(f32[1]{0:T(128)} %add.45), channel_id=1, source_target_pairs={{0,128},{64,192},{128,0},{192,64},{1,129},{65,193},{129,1},{193,65... | collective-permute-start | bytes 20 | tf_op jit(solution)/shard_map/ppermute | solution.py:20
  167.7 3.8 %collective-permute-done.16 = f32[1]{0:T(128)} collective-permute-done((f32[1]{0:T(128)}, f32[1]{0:T(128)}, u32[]{:S(2)}, u32[]{:S(2)}) %collective-permute-start.16) | collective-permute-done | bytes 36 | tf_op jit(solution)/shard_map/ppermute | solution.py:20
  172.1 3.2 %collective-permute-start.17 = (f32[1]{0:T(128)}, f32[1]{0:T(128)}, u32[]{:S(2)}, u32[]{:S(2)}) collective-permute-start(f32[1]{0:T(128)} %add.46), channel_id=1, source_target_pairs={{0,4},{4,8},{8,12},{12,16},{16,20},{20,24},{24,28},{28,32},{32,36}... | collective-permute-start | bytes 20 | tf_op jit(solution)/shard_map/ppermute | solution.py:20
  175.3 3.5 %collective-permute-done.17 = f32[1]{0:T(128)} collective-permute-done((f32[1]{0:T(128)}, f32[1]{0:T(128)}, u32[]{:S(2)}, u32[]{:S(2)}) %collective-permute-start.17) | collective-permute-done | bytes 36 | tf_op jit(solution)/shard_map/ppermute | solution.py:20
  179.4 3.2 %collective-permute-start.18 = (f32[1]{0:T(128)}, f32[1]{0:T(128)}, u32[]{:S(2)}, u32[]{:S(2)}) collective-permute-start(f32[1]{0:T(128)} %add.47), channel_id=1, source_target_pairs={{0,8},{4,12},{8,16},{12,20},{16,24},{20,28},{24,32},{28,36},{32,40... | collective-permute-start | bytes 20 | tf_op jit(solution)/shard_map/ppermute | solution.py:20
  182.6 4.4 %collective-permute-done.18 = f32[1]{0:T(128)} collective-permute-done((f32[1]{0:T(128)}, f32[1]{0:T(128)}, u32[]{:S(2)}, u32[]{:S(2)}) %collective-permute-start.18) | collective-permute-done | bytes 36 | tf_op jit(solution)/shard_map/ppermute | solution.py:20
  187.7 3.2 %collective-permute-start.19 = (f32[1]{0:T(128)}, f32[1]{0:T(128)}, u32[]{:S(2)}, u32[]{:S(2)}) collective-permute-start(f32[1]{0:T(128)} %add.48), channel_id=1, source_target_pairs={{0,16},{4,20},{8,24},{12,28},{16,32},{20,36},{24,40},{28,44},{32,4... | collective-permute-start | bytes 20 | tf_op jit(solution)/shard_map/ppermute | solution.py:20
  190.9 6.2 %collective-permute-done.19 = f32[1]{0:T(128)} collective-permute-done((f32[1]{0:T(128)}, f32[1]{0:T(128)}, u32[]{:S(2)}, u32[]{:S(2)}) %collective-permute-start.19) | collective-permute-done | bytes 36 | tf_op jit(solution)/shard_map/ppermute | solution.py:20
  197.7 3.2 %collective-permute-start.20 = (f32[1]{0:T(128)}, f32[1]{0:T(128)}, u32[]{:S(2)}, u32[]{:S(2)}) collective-permute-start(f32[1]{0:T(128)} %add.49), channel_id=1, source_target_pairs={{0,32},{4,36},{8,40},{12,44},{16,48},{20,52},{24,56},{28,60},{32,0... | collective-permute-start | bytes 20 | tf_op jit(solution)/shard_map/ppermute | solution.py:20
  200.9 11.1 %collective-permute-done.20 = f32[1]{0:T(128)} collective-permute-done((f32[1]{0:T(128)}, f32[1]{0:T(128)}, u32[]{:S(2)}, u32[]{:S(2)}) %collective-permute-start.20) | collective-permute-done | bytes 36 | tf_op jit(solution)/shard_map/ppermute | solution.py:20
  (17 shorter events, 0.3 us)
Async XLA Ops:
  0.6 35.8 %collective-permute-start = (bf16[384,1152]{1,0:T(8,128)(2,1)}, bf16[384,1152]{1,0:T(8,128)(2,1)}, u32[]{:S(2)}, u32[]{:S(2)}) collective-permute-start(bf16[384,1152]{1,0:T(8,128)(2,1)} %refs_2_.1), channel_id=1, source_target_pairs={{0,508},{4,0},{8,4},{12,8},{16,12},{20,16},{24,20},{28,24},{32,28}... | collective-permute-start | bytes 2654216 | tf_op jit(solution)/shard_map/ppermute | solution.py:20
  16.1 30.5 %collective-permute-start.1 = (bf16[384,1152]{1,0:T(8,128)(2,1)}, bf16[384,1152]{1,0:T(8,128)(2,1)}, u32[]{:S(2)}, u32[]{:S(2)}) collective-permute-start(bf16[384,1152]{1,0:T(8,128)(2,1)} %refs_2_.1), channel_id=1, source_target_pairs={{0,4},{4,8},{8,12},{12,16},{16,20},{20,24},{24,28},{28,32},{32,36}... | collective-permute-start | bytes 2654216 | tf_op jit(solution)/shard_map/ppermute | solution.py:20
  18.0 37.4 %collective-permute-start.6 = (bf16[384,1152]{1,0:T(8,128)(2,1)}, bf16[384,1152]{1,0:T(8,128)(2,1)S(1)}, u32[]{:S(2)}, u32[]{:S(2)}) collective-permute-start(bf16[384,1152]{1,0:T(8,128)(2,1)} %refs_3_.1), channel_id=1, source_target_pairs={{0,508},{4,0},{8,4},{12,8},{16,12},{20,16},{24,20},{28,24},{32,28}... | collective-permute-start | bytes 2654216 | tf_op jit(solution)/shard_map/ppermute | solution.py:20
  27.6 37.8 %collective-permute-start.7 = (bf16[384,1152]{1,0:T(8,128)(2,1)}, bf16[384,1152]{1,0:T(8,128)(2,1)S(1)}, u32[]{:S(2)}, u32[]{:S(2)}) collective-permute-start(bf16[384,1152]{1,0:T(8,128)(2,1)} %refs_3_.1), channel_id=1, source_target_pairs={{0,4},{4,8},{8,12},{12,16},{16,20},{20,24},{24,28},{28,32},{32,36}... | collective-permute-start | bytes 2654216 | tf_op jit(solution)/shard_map/ppermute | solution.py:20
  36.4 37.9 %collective-permute-start.2 = (bf16[384,1152]{1,0:T(8,128)(2,1)}, bf16[384,1152]{1,0:T(8,128)(2,1)}, u32[]{:S(2)}, u32[]{:S(2)}) collective-permute-start(bf16[384,1152]{1,0:T(8,128)(2,1)} %collective-permute-done.refs_3_), channel_id=1, source_target_pairs={{0,508},{4,0},{8,4},{12,8},{16,12},{20,16},{24,20},{28,24},{32,28}... | collective-permute-start | bytes 2654216 | tf_op jit(solution)/shard_map/ppermute | solution.py:20
  46.6 37.9 %collective-permute-start.3 = (bf16[384,1152]{1,0:T(8,128)(2,1)}, bf16[384,1152]{1,0:T(8,128)(2,1)}, u32[]{:S(2)}, u32[]{:S(2)}) collective-permute-start(bf16[384,1152]{1,0:T(8,128)(2,1)} %collective-permute-done.1.refs_4_), channel_id=1, source_target_pairs={{0,4},{4,8},{8,12},{12,16},{16,20},{20,24},{24,28},{28,32},{32,36}... | collective-permute-start | bytes 2654216 | tf_op jit(solution)/shard_map/ppermute | solution.py:20
  55.4 37.8 %collective-permute-start.8 = (bf16[384,1152]{1,0:T(8,128)(2,1)S(1)}, bf16[384,1152]{1,0:T(8,128)(2,1)S(1)}, u32[]{:S(2)}, u32[]{:S(2)}) collective-permute-start(bf16[384,1152]{1,0:T(8,128)(2,1)S(1)} %collective-permute-done.6.refs_2_), channel_id=1, source_target_pairs={{0,508},{4,0},{8,4},{12,8},{16,12},{20,16},{24,20},{28,24},{32,28}... | collective-permute-start | bytes 2654216 | tf_op jit(solution)/shard_map/ppermute | solution.py:20
  65.4 37.9 %collective-permute-start.9 = (bf16[384,1152]{1,0:T(8,128)(2,1)S(1)}, bf16[384,1152]{1,0:T(8,128)(2,1)S(1)}, u32[]{:S(2)}, u32[]{:S(2)}) collective-permute-start(bf16[384,1152]{1,0:T(8,128)(2,1)S(1)} %collective-permute-done.7.refs_3_), channel_id=1, source_target_pairs={{0,4},{4,8},{8,12},{12,16},{16,20},{20,24},{24,28},{28,32},{32,36}... | collective-permute-start | bytes 2654216 | tf_op jit(solution)/shard_map/ppermute | solution.py:20
  74.3 46.4 %collective-permute-start.4 = (bf16[384,1152]{1,0:T(8,128)(2,1)}, bf16[384,1152]{1,0:T(8,128)(2,1)S(1)}, u32[]{:S(2)}, u32[]{:S(2)}) collective-permute-start(bf16[384,1152]{1,0:T(8,128)(2,1)} %collective-permute-done.2.refs_3_), channel_id=1, source_target_pairs={{0,508},{4,0},{8,4},{12,8},{16,12},{20,16},{24,20},{28,24},{32,28}... | collective-permute-start | bytes 2654216 | tf_op jit(solution)/shard_map/ppermute | solution.py:20
  84.5 37.8 %collective-permute-start.5 = (bf16[384,1152]{1,0:T(8,128)(2,1)}, bf16[384,1152]{1,0:T(8,128)(2,1)S(1)}, u32[]{:S(2)}, u32[]{:S(2)}) collective-permute-start(bf16[384,1152]{1,0:T(8,128)(2,1)} %collective-permute-done.3.refs_4_), channel_id=1, source_target_pairs={{0,4},{4,8},{8,12},{12,16},{16,20},{20,24},{24,28},{28,32},{32,36}... | collective-permute-start | bytes 2654216 | tf_op jit(solution)/shard_map/ppermute | solution.py:20
  93.2 36.8 %collective-permute-start.10 = (bf16[384,1152]{1,0:T(8,128)(2,1)S(1)}, bf16[384,1152]{1,0:T(8,128)(2,1)S(1)}, u32[]{:S(2)}, u32[]{:S(2)}) collective-permute-start(bf16[384,1152]{1,0:T(8,128)(2,1)S(1)} %collective-permute-done.8.refs_2_), channel_id=1, source_target_pairs={{0,508},{4,0},{8,4},{12,8},{16,12},{20,16},{24,20},{28,24},{32,28}... | collective-permute-start | bytes 2654216 | tf_op jit(solution)/shard_map/ppermute | solution.py:20
  103.3 36.5 %collective-permute-start.11 = (bf16[384,1152]{1,0:T(8,128)(2,1)S(1)}, bf16[384,1152]{1,0:T(8,128)(2,1)S(1)}, u32[]{:S(2)}, u32[]{:S(2)}) collective-permute-start(bf16[384,1152]{1,0:T(8,128)(2,1)S(1)} %collective-permute-done.9.refs_3_), channel_id=1, source_target_pairs={{0,4},{4,8},{8,12},{12,16},{16,20},{20,24},{24,28},{28,32},{32,36}... | collective-permute-start | bytes 2654216 | tf_op jit(solution)/shard_map/ppermute | solution.py:20
  105.3 1.2 copy-start
  106.5 1.2 copy-start.2
  107.7 0.7 copy-start.4
  117.8 4.5 %copy-start.1 = (bf16[384,1152]{1,0:T(8,128)(2,1)S(1)}, bf16[384,1152]{1,0:T(8,128)(2,1)}, u32[]{:S(2)}) copy-start(bf16[384,1152]{1,0:T(8,128)(2,1)} %refs_3_.1) | copy-start | bytes 2654212
  122.3 17.5 %copy-start.3 = (bf16[384,1152]{1,0:T(8,128)(2,1)S(1)}, bf16[384,1152]{1,0:T(8,128)(2,1)}, u32[]{:S(2)}) copy-start(bf16[384,1152]{1,0:T(8,128)(2,1)} %refs_2_.1) | copy-start | bytes 2654212
  127.0 15.2 %collective-permute-start.12 = (f32[1]{0:T(128)}, f32[1]{0:T(128)}, u32[]{:S(2)}, u32[]{:S(2)}) collective-permute-start(f32[1]{0:T(128)} %get-tuple-element.24), channel_id=1, source_target_pairs={{0,1},{1,0},{2,3},{3,2},{4,5},{5,4},{6,7},{7,6},{8,9},{9,8},{10,11... | collective-permute-start | bytes 20 | tf_op jit(solution)/shard_map/ppermute | solution.py:20
  143.4 5.5 %collective-permute-start.13 = (f32[1]{0:T(128)}, f32[1]{0:T(128)}, u32[]{:S(2)}, u32[]{:S(2)}) collective-permute-start(f32[1]{0:T(128)} %add.42), channel_id=1, source_target_pairs={{0,2},{2,0},{1,3},{3,1},{4,6},{6,4},{5,7},{7,5},{8,10},{10,8},{9,1... | collective-permute-start | bytes 20 | tf_op jit(solution)/shard_map/ppermute | solution.py:20
  149.5 7.0 %collective-permute-start.14 = (f32[1]{0:T(128)}, f32[1]{0:T(128)}, u32[]{:S(2)}, u32[]{:S(2)}) collective-permute-start(f32[1]{0:T(128)} %add.43), channel_id=1, source_target_pairs={{0,256},{256,0},{1,257},{257,1},{2,258},{258,2},{3,259},{259,3},{4... | collective-permute-start | bytes 20 | tf_op jit(solution)/shard_map/ppermute | solution.py:20
  157.2 6.8 %collective-permute-start.15 = (f32[1]{0:T(128)}, f32[1]{0:T(128)}, u32[]{:S(2)}, u32[]{:S(2)}) collective-permute-start(f32[1]{0:T(128)} %add.44), channel_id=1, source_target_pairs={{0,64},{64,128},{128,192},{192,0},{1,65},{65,129},{129,193},{193,1... | collective-permute-start | bytes 20 | tf_op jit(solution)/shard_map/ppermute | solution.py:20
  164.5 7.0 %collective-permute-start.16 = (f32[1]{0:T(128)}, f32[1]{0:T(128)}, u32[]{:S(2)}, u32[]{:S(2)}) collective-permute-start(f32[1]{0:T(128)} %add.45), channel_id=1, source_target_pairs={{0,128},{64,192},{128,0},{192,64},{1,129},{65,193},{129,1},{193,65... | collective-permute-start | bytes 20 | tf_op jit(solution)/shard_map/ppermute | solution.py:20
  172.1 6.8 %collective-permute-start.17 = (f32[1]{0:T(128)}, f32[1]{0:T(128)}, u32[]{:S(2)}, u32[]{:S(2)}) collective-permute-start(f32[1]{0:T(128)} %add.46), channel_id=1, source_target_pairs={{0,4},{4,8},{8,12},{12,16},{16,20},{20,24},{24,28},{28,32},{32,36}... | collective-permute-start | bytes 20 | tf_op jit(solution)/shard_map/ppermute | solution.py:20
  179.4 7.6 %collective-permute-start.18 = (f32[1]{0:T(128)}, f32[1]{0:T(128)}, u32[]{:S(2)}, u32[]{:S(2)}) collective-permute-start(f32[1]{0:T(128)} %add.47), channel_id=1, source_target_pairs={{0,8},{4,12},{8,16},{12,20},{16,24},{20,28},{24,32},{28,36},{32,40... | collective-permute-start | bytes 20 | tf_op jit(solution)/shard_map/ppermute | solution.py:20
  187.7 9.4 %collective-permute-start.19 = (f32[1]{0:T(128)}, f32[1]{0:T(128)}, u32[]{:S(2)}, u32[]{:S(2)}) collective-permute-start(f32[1]{0:T(128)} %add.48), channel_id=1, source_target_pairs={{0,16},{4,20},{8,24},{12,28},{16,32},{20,36},{24,40},{28,44},{32,4... | collective-permute-start | bytes 20 | tf_op jit(solution)/shard_map/ppermute | solution.py:20
  197.7 14.3 %collective-permute-start.20 = (f32[1]{0:T(128)}, f32[1]{0:T(128)}, u32[]{:S(2)}, u32[]{:S(2)}) collective-permute-start(f32[1]{0:T(128)} %add.49), channel_id=1, source_target_pairs={{0,32},{4,36},{8,40},{12,44},{16,48},{20,52},{24,56},{28,60},{32,0... | collective-permute-start | bytes 20 | tf_op jit(solution)/shard_map/ppermute | solution.py:20

commit v2 on v1

--- a/solution.py
+++ b/solution.py
@@ -12,7 +12,7 @@
 BLK = ("x_hi", "y", "z")
 
 EPSILON = 1e-06
-VMEM_LIMIT = 32 * 1024 * 1024
+VMEM_LIMIT = 16 * 1024 * 1024
 
 
 def shifted(value, axis, steps):
@@ -34,6 +34,12 @@
     small = jnp.exp(-jnp.abs(u))
     loss = jnp.maximum(u, 0.0) + jnp.log1p(small)
     return loss, jnp.where(u >= 0.0, 1.0, small) / (1.0 + small)
+
+
+def grad_of(raw, upstream):
+    unit, inverse = unit_of(raw)
+    inward = jnp.sum(unit * upstream, axis=1, keepdims=True)
+    return ((upstream - unit * inward) * inverse).astype(jnp.bfloat16)
 
 
 def own_kernel(scal, positives, image, text, image_half, text_half, image_acc, text_acc, loss):
@@ -57,9 +63,10 @@
     out = refs.pop(0)
     loss_out = refs.pop(0) if with_loss else None
     total = refs.pop(0) if last else out
+    loss = refs.pop(0) if with_loss and last else loss_out
     total[...] = acc[...]
     if with_loss:
-        loss_out[0] = loss_in[0]
+        loss[0] = loss_in[0]
     for (row, column), partner in zip(which, partners):
 
         @pl.when(flags[row, column] > 0)
@@ -68,19 +75,22 @@
             z = scal[0] * dot(half[...], other, (1, 1)) + scal[1]
             part, sigmoid = loss_and_sigmoid(z)
             if with_loss:
-                loss_out[0] = loss_out[0] + jnp.sum(part)
+                loss[0] = loss[0] + jnp.sum(part)
             slopes = (sigmoid * scal[0]).astype(jnp.bfloat16)
             total[...] += dot(slopes, other, (1, 0))
 
     if last:
-        unit, inverse = unit_of(raw[...])
-        upstream = total[...]
-        inward = jnp.sum(unit * upstream, axis=1, keepdims=True)
-        out[...] = ((upstream - unit * inward) * inverse).astype(jnp.bfloat16)
+        out[...] = grad_of(raw[...], total[...])
+        if with_loss:
+            loss_out[...] = jnp.full(loss_out.shape, loss[0], jnp.float32)
+
+
+def total_kernel(received, out):
+    out[...] = jnp.broadcast_to(jnp.sum(received[...], axis=0, keepdims=True), out.shape)
 
 
 SMEM = pl.BlockSpec(memory_space=pltpu.SMEM)
-VMEM = pl.BlockSpec(memory_space=pltpu.VMEM)
+VMEM = pl.BlockSpec()
 
 
 def cost(pairs, blocks):
@@ -100,22 +110,22 @@
     )(scal, positives, image, text)
 
 
-def add_pairs(which, flags, scal, loss, half, acc, raw, partners, name):
+def add_pairs(which, flags, scal, loss, half, acc, raw, partners, name, copies=0):
     with_loss, last = loss is not None, raw is not None
     operands = [flags, scal] + ([loss] if with_loss else []) + [half, acc] + ([raw] if last else []) + list(partners)
     in_specs = [SMEM, SMEM] + ([SMEM] if with_loss else []) + [VMEM] * (2 + last + len(partners))
     out_shape = [jax.ShapeDtypeStruct(acc.shape, jnp.bfloat16 if last else jnp.float32)]
     out_specs = [VMEM]
     if with_loss:
-        out_shape.append(jax.ShapeDtypeStruct((1,), jnp.float32))
-        out_specs.append(SMEM)
+        out_shape.append(jax.ShapeDtypeStruct((copies, 1, 128) if last else (1,), jnp.float32))
+        out_specs.append(VMEM if last else SMEM)
     aliases = {} if last else {3 + with_loss: 0}
     return pl.pallas_call(
         functools.partial(pair_kernel, tuple(which), with_loss, last),
         out_shape=out_shape,
         in_specs=in_specs,
         out_specs=out_specs,
-        scratch_shapes=[pltpu.VMEM(acc.shape, jnp.float32)] if last else [],
+        scratch_shapes=([pltpu.VMEM(acc.shape, jnp.float32)] + [pltpu.SMEM((1,), jnp.float32)] * with_loss) if last else [],
         input_output_aliases=aliases,
         compiler_params=pltpu.CompilerParams(vmem_limit_bytes=VMEM_LIMIT),
         cost_estimate=cost(len(partners), 6 + len(partners)),
@@ -133,13 +143,23 @@
     return jnp.stack([mine, theirs])
 
 
-def summed(value):
-    for axis in ("core", "x_lo", "x_hi", "y", "z"):
-        step = 1
-        while step < lax.axis_size(axis):
-            value = value + shifted(value, axis, step)
-            step *= 2
-    return value
+def exchanged(values, axes):
+    return lax.all_to_all(values, axes, 0, 0, tiled=True)
+
+
+def totals(received, copies):
+    return pl.pallas_call(
+        total_kernel,
+        out_shape=jax.ShapeDtypeStruct((copies, 1, 128), jnp.float32),
+        in_specs=[VMEM],
+        out_specs=VMEM,
+        compiler_params=pltpu.CompilerParams(vmem_limit_bytes=VMEM_LIMIT),
+        name="plane_total",
+    )(received)
+
+
+def after(value, *others):
+    return lax.optimization_barrier((value, *others))[0]
 
 
 def body(image_emb, text_emb, positives, pair_mask, log_scale, bias):
@@ -147,26 +167,37 @@
     scal = jnp.concatenate([jnp.exp(log_scale), bias])
     flags = flags_of(pair_mask, reach)
 
-    texts, images = {0: text_emb}, {0: image_emb}
-    for distance in range(1, reach + 1):
-        for held in (texts, images):
-            for sign in (1, -1):
-                held[sign * distance] = shifted(held[sign * (distance - 1)], BLK, -sign)
-
-    image_half, text_half, image_acc, text_acc, loss = own_pair(scal, positives, image_emb, text_emb)
-    for d in range(1, reach + 1):
-        last = d == reach
-        image_acc, loss = add_pairs(
-            [(0, reach + d), (0, reach - d)], flags, scal, loss, image_half, image_acc,
-            image_emb if last else None, [texts[d], texts[-d]], f"image_side_{d}",
-        )
-        (text_acc,) = add_pairs(
-            [(1, reach - d), (1, reach + d)], flags, scal, None, text_half, text_acc,
-            text_emb if last else None, [images[d], images[-d]], f"text_side_{d}",
-        )
-    total = summed(loss)
+    def sent_on(held, *token):
+        return [shifted(after(held[0], *token), BLK, 1), shifted(after(held[1], *token), BLK, -1)]
+
+    def image_side(d, loss, acc, partners, raw=None, copies=0):
+        which = [(0, reach + d), (0, reach - d)]
+        return add_pairs(which, flags, scal, loss, image_half, acc, raw, partners[::-1], f"image_side_{d}", copies)
+
+    def text_side(d, acc, partners, name, raw=None):
+        which = [(1, reach - d), (1, reach + d)]
+        return add_pairs(which, flags, scal, None, text_half, acc, raw, partners[::-1], f"text_side_{name}")[0]
+
+    texts_1 = sent_on([text_emb, text_emb])
+    images_1 = sent_on([image_emb, image_emb])
+    image_half, text_half, image_acc, text_acc, loss_0 = own_pair(scal, positives, image_emb, text_emb)
+    texts_2 = sent_on(texts_1, loss_0)
+    image_acc, loss_1 = image_side(1, loss_0, image_acc, texts_1)
+    images_2 = sent_on(images_1, loss_1)
+    text_acc = text_side(1, text_acc, images_1, "1")
+    texts_3 = sent_on(texts_2, text_acc)
+    image_acc, loss_2 = image_side(2, loss_1, image_acc, texts_2)
+    images_3 = sent_on(images_2, loss_2)
+    text_acc = text_side(2, text_acc, images_2, "2")
+    plane, line = ("x_hi", "y", "x_lo", "core"), ("z",)
+    image_grad, losses = image_side(
+        3, after(loss_2, text_acc), image_acc, texts_3, image_emb, lax.axis_size(plane)
+    )
+    sums = totals(exchanged(losses, plane), lax.axis_size(line))
+    total = jnp.sum(exchanged(sums, line)[:, 0, 0]).reshape(1)
+    text_grad = text_side(3, after(text_acc, sums), images_3, "3", text_emb)
     image_count = image_emb.shape[0] * lax.axis_size(ALL)
-    return image_acc, text_acc, total / image_count
+    return image_grad, text_grad, total / image_count
 
 
 def solution(mesh):

time: 215 us -> 155 us (0.72)
  the two profiles are of different devices: /device:TPU:2 before, /device:TPU:1 now
where the time goes in v2:
time: 155 us; the launch traced here: 154 us
  starting transfers between devices  80.3 us (52%)
  Pallas kernels  24.7 us (16%)
  waiting for transfers between devices  22.6 us (15%)
  blocking collectives  17.7 us (11%)
  between operations  3.98 us (3%)
  local copies, waits for them, and re-layouts  3.02 us (2%)
  other arithmetic  1.63 us (1%)
    ppermute x12, starting transfers between devices, shifted(): lax.ppermute(value, axis, [(s, (s + steps) % count) for s in range(count)])  74.9 us
    pallas_call x6, Pallas kernels, add_pairs(): pl.pallas_call(functools.partial(pair_kernel, tuple(which), with_loss, la...  20.9 us
    all_to_all x1, blocking collectives, exchanged(): return lax.all_to_all(values, axes, 0, 0, tiled=True)  17.7 us
    ppermute x12, waiting for transfers between devices, shifted(): lax.ppermute(value, axis, [(s, (s + steps) % count) for s in range(count)])  16.4 us
    all_to_all x1, waiting for transfers between devices, exchanged(): return lax.all_to_all(values, axes, 0, 0, tiled=True)  6.17 us
    all_to_all x1, starting transfers between devices, exchanged(): return lax.all_to_all(values, axes, 0, 0, tiled=True)  5.38 us
    pallas_call x1, Pallas kernels, own_pair(): pl.pallas_call(own_kernel, out_shape=[jax.ShapeDtypeStruct(shape, jnp.bfl...  3.19 us
  transfers between devices with their start and end apart: 13, of which 7 were waited for; matrix products, arithmetic and copies ran while one was open for 1% of the time, Pallas kernels for 16%

profile of v2, /device:TPU:1, one launch (start us, length us, event | category | flops | bytes accessed | tf_op | source)
XLA Modules:
  0.0 153.9 jit_solution(348151571939722485)
XLA Ops:
  0.6 4.4 %collective-permute-start.1 = (bf16[384,1152]{1,0:T(8,128)(2,1)}, bf16[384,1152]{1,0:T(8,128)(2,1)}, u32[]{:S(2)}, u32[]{:S(2)}) collective-permute-start(bf16[384,1152]{1,0:T(8,128)(2,1)} %refs_2_.1), channel_id=1, source_target_pairs={{0,4},{4,8},{8,12},{12,16},{16,20},{20,24},{24,28},{28,32},{32,36}... | collective-permute-start | bytes 2654216 | tf_op jit(solution)/shard_map/ppermute | solution.py:20
  5.0 14.4 %collective-permute-start = (bf16[384,1152]{1,0:T(8,128)(2,1)}, bf16[384,1152]{1,0:T(8,128)(2,1)}, u32[]{:S(2)}, u32[]{:S(2)}) collective-permute-start(bf16[384,1152]{1,0:T(8,128)(2,1)} %refs_2_.1), channel_id=1, source_target_pairs={{0,508},{4,0},{8,4},{12,8},{16,12},{20,16},{24,20},{28,24},{32,28}... | collective-permute-start | bytes 2654216 | tf_op jit(solution)/shard_map/ppermute | solution.py:20
  19.4 1.9 %collective-permute-start.5 = (bf16[384,1152]{1,0:T(8,128)(2,1)}, bf16[384,1152]{1,0:T(8,128)(2,1)S(1)}, u32[]{:S(2)}, u32[]{:S(2)}) collective-permute-start(bf16[384,1152]{1,0:T(8,128)(2,1)} %refs_3_.1), channel_id=1, source_target_pairs={{0,4},{4,8},{8,12},{12,16},{16,20},{20,24},{24,28},{28,32},{32,36}... | collective-permute-start | bytes 2654216 | tf_op jit(solution)/shard_map/ppermute | solution.py:20
  21.4 9.1 %collective-permute-start.4 = (bf16[384,1152]{1,0:T(8,128)(2,1)}, bf16[384,1152]{1,0:T(8,128)(2,1)}, u32[]{:S(2)}, u32[]{:S(2)}) collective-permute-start(bf16[384,1152]{1,0:T(8,128)(2,1)} %refs_3_.1), channel_id=1, source_target_pairs={{0,508},{4,0},{8,4},{12,8},{16,12},{20,16},{24,20},{28,24},{32,28}... | collective-permute-start | bytes 2654216 | tf_op jit(solution)/shard_map/ppermute | solution.py:20
  31.8 0.1 pad_maximum_fusion.scal
  31.9 0.9 select_reduce_fusion.1
  32.8 0.0 copy-start
  32.8 1.2 copy-done
  34.0 0.0 copy-start.2
  34.0 1.2 copy-done.2
  35.2 0.0 copy-start.4
  35.2 0.7 copy-done.4
  35.8 3.2 %own_pair.1 = (bf16[384,1152]{1,0:T(8,128)(2,1)S(1)}, bf16[384,1152]{1,0:T(8,128)(2,1)S(1)}, f32[384,1152]{1,0:T(8,128)S(1)}, f32[384,1152]{1,0:T(8,128)S(1)}, f32[1]{0:T(128)}) custom-call(f32[2]{0:T(128)S(1)} %pad_maximum_fusion.scal, s32[1,384]{1,0:T(1,128)S(1)} %copy-done.4, bf16[384,1152]{1,0:T(8,128)(2,1)S(1)} %copy-done, bf16[384,1152]{1,0:T(8,128)(2,1)S(1)} %copy-done.2), custom_call_target="tpu_custom_call" | custom-call | flops 1358954496 | bytes 7077888 | tf_op jit(solution)/shard_map/own_pair/pallas_call | solution.py:102
  39.0 0.0 collective-permute-done.1.refs_4_
  39.1 0.0 collective-permute-done.refs_3_
  39.1 8.8 %collective-permute-start.2 = (bf16[384,1152]{1,0:T(8,128)(2,1)}, bf16[384,1152]{1,0:T(8,128)(2,1)S(1)}, u32[]{:S(2)}, u32[]{:S(2)}) collective-permute-start(bf16[384,1152]{1,0:T(8,128)(2,1)} %collective-permute-done.refs_3_), channel_id=1, source_target_pairs={{0,508},{4,0},{8,4},{12,8},{16,12},{20,16},{24,20},{28,24},{32,28}... | collective-permute-start | bytes 2654216 | tf_op jit(solution)/shard_map/ppermute | solution.py:20
  47.9 1.9 %collective-permute-start.3 = (bf16[384,1152]{1,0:T(8,128)(2,1)}, bf16[384,1152]{1,0:T(8,128)(2,1)S(1)}, u32[]{:S(2)}, u32[]{:S(2)}) collective-permute-start(bf16[384,1152]{1,0:T(8,128)(2,1)} %collective-permute-done.1.refs_4_), channel_id=1, source_target_pairs={{0,4},{4,8},{8,12},{12,16},{16,20},{20,24},{24,28},{28,32},{32,36}... | collective-permute-start | bytes 2654216 | tf_op jit(solution)/shard_map/ppermute | solution.py:20
  49.8 2.8 %image_side_1.1 = (f32[384,1152]{1,0:T(8,128)S(1)}, f32[1]{0:T(128)}) custom-call(s32[2,7]{1,0:T(2,128)S(1)} %pad_add_fusion.flags, f32[2]{0:T(128)S(1)} %pad_maximum_fusion.scal, f32[1]{0:T(128)} %get-tuple-element.24.refs_0_, bf16[384,1152]{1,0:T(8,128)(2,1)S(1)} %get-tuple-element.25.refs_1_, ...), custom_call_target="tpu_custom_call", output_to_operand_aliasing={{0}: (4, {})} | custom-call | flops 1358954496 | bytes 7077888 | tf_op jit(solution)/shard_map/image_side_1/pallas_call | solution.py:123
  52.7 3.4 %collective-permute-done.5.refs_3_ = bf16[384,1152]{1,0:T(8,128)(2,1)S(1)} collective-permute-done((bf16[384,1152]{1,0:T(8,128)(2,1)}, bf16[384,1152]{1,0:T(8,128)(2,1)S(1)}, u32[]{:S(2)}, u32[]{:S(2)}) %collective-permute-start.5) | collective-permute-done | bytes 884768 | tf_op jit(solution)/shard_map/ppermute | solution.py:20
  56.0 1.9 %collective-permute-start.7 = (bf16[384,1152]{1,0:T(8,128)(2,1)S(1)}, bf16[384,1152]{1,0:T(8,128)(2,1)}, u32[]{:S(2)}, u32[]{:S(2)}) collective-permute-start(bf16[384,1152]{1,0:T(8,128)(2,1)S(1)} %collective-permute-done.5.refs_3_), channel_id=1, source_target_pairs={{0,4},{4,8},{8,12},{12,16},{16,20},{20,24},{24,28},{28,32},{32,36}... | collective-permute-start | bytes 2654216 | tf_op jit(solution)/shard_map/ppermute | solution.py:20
  58.0 0.0 collective-permute-done.4.refs_2_
  58.0 9.1 %collective-permute-start.6 = (bf16[384,1152]{1,0:T(8,128)(2,1)}, bf16[384,1152]{1,0:T(8,128)(2,1)}, u32[]{:S(2)}, u32[]{:S(2)}) collective-permute-start(bf16[384,1152]{1,0:T(8,128)(2,1)} %collective-permute-done.4.refs_2_), channel_id=1, source_target_pairs={{0,508},{4,0},{8,4},{12,8},{16,12},{20,16},{24,20},{28,24},{32,28}... | collective-permute-start | bytes 2654216 | tf_op jit(solution)/shard_map/ppermute | solution.py:20
  67.1 1.4 text_side_1.1.refs_1_
  68.5 5.4 %collective-permute-done.3.refs_4_ = bf16[384,1152]{1,0:T(8,128)(2,1)S(1)} collective-permute-done((bf16[384,1152]{1,0:T(8,128)(2,1)}, bf16[384,1152]{1,0:T(8,128)(2,1)S(1)}, u32[]{:S(2)}, u32[]{:S(2)}) %collective-permute-start.3) | collective-permute-done | bytes 884768 | tf_op jit(solution)/shard_map/ppermute | solution.py:20
  73.9 2.1 %collective-permute-done.2.refs_3_ = bf16[384,1152]{1,0:T(8,128)(2,1)S(1)} collective-permute-done((bf16[384,1152]{1,0:T(8,128)(2,1)}, bf16[384,1152]{1,0:T(8,128)(2,1)S(1)}, u32[]{:S(2)}, u32[]{:S(2)}) %collective-permute-start.2) | collective-permute-done | bytes 884768 | tf_op jit(solution)/shard_map/ppermute | solution.py:20
  76.0 9.7 %collective-permute-start.8 = (bf16[384,1152]{1,0:T(8,128)(2,1)S(1)}, bf16[384,1152]{1,0:T(8,128)(2,1)S(1)}, u32[]{:S(2)}, u32[]{:S(2)}) collective-permute-start(bf16[384,1152]{1,0:T(8,128)(2,1)S(1)} %collective-permute-done.2.refs_3_), channel_id=1, source_target_pairs={{0,508},{4,0},{8,4},{12,8},{16,12},{20,16},{24,20},{28,24},{32,28}... | collective-permute-start | bytes 2654216 | tf_op jit(solution)/shard_map/ppermute | solution.py:20
  85.7 1.9 %collective-permute-start.9 = (bf16[384,1152]{1,0:T(8,128)(2,1)S(1)}, bf16[384,1152]{1,0:T(8,128)(2,1)S(1)}, u32[]{:S(2)}, u32[]{:S(2)}) collective-permute-start(bf16[384,1152]{1,0:T(8,128)(2,1)S(1)} %collective-permute-done.3.refs_4_), channel_id=1, source_target_pairs={{0,4},{4,8},{8,12},{12,16},{16,20},{20,24},{24,28},{28,32},{32,36}... | collective-permute-start | bytes 2654216 | tf_op jit(solution)/shard_map/ppermute | solution.py:20
  87.6 4.0 %image_side_2.1 = (f32[384,1152]{1,0:T(8,128)S(1)}, f32[1]{0:T(128)}) custom-call(s32[2,7]{1,0:T(2,128)S(1)} %pad_add_fusion.flags, f32[2]{0:T(128)S(1)} %pad_maximum_fusion.scal, f32[1]{0:T(128)} %get-tuple-element.27.refs_0_, bf16[384,1152]{1,0:T(8,128)(2,1)S(1)} %get-tuple-element.25.refs_1_, ...), custom_call_target="tpu_custom_call", output_to_operand_aliasing={{0}: (4, {})} | custom-call | flops 1358954496 | bytes 7077888 | tf_op jit(solution)/shard_map/image_side_2/pallas_call | solution.py:123
  91.6 1.3 collective-permute-done.7.refs_3_
  92.9 0.0 copy-start.1
  92.9 2.0 %collective-permute-done.6.refs_2_ = bf16[384,1152]{1,0:T(8,128)(2,1)} collective-permute-done((bf16[384,1152]{1,0:T(8,128)(2,1)}, bf16[384,1152]{1,0:T(8,128)(2,1)}, u32[]{:S(2)}, u32[]{:S(2)}) %collective-permute-start.6) | collective-permute-done | bytes 884768 | tf_op jit(solution)/shard_map/ppermute | solution.py:20
  94.9 9.8 %collective-permute-start.10 = (bf16[384,1152]{1,0:T(8,128)(2,1)}, bf16[384,1152]{1,0:T(8,128)(2,1)}, u32[]{:S(2)}, u32[]{:S(2)}) collective-permute-start(bf16[384,1152]{1,0:T(8,128)(2,1)} %collective-permute-done.6.refs_2_), channel_id=1, source_target_pairs={{0,508},{4,0},{8,4},{12,8},{16,12},{20,16},{24,20},{28,24},{32,28}... | collective-permute-start | bytes 2654216 | tf_op jit(solution)/shard_map/ppermute | solution.py:20
  104.8 1.9 %collective-permute-start.11 = (bf16[384,1152]{1,0:T(8,128)(2,1)}, bf16[384,1152]{1,0:T(8,128)(2,1)}, u32[]{:S(2)}, u32[]{:S(2)}) collective-permute-start(bf16[384,1152]{1,0:T(8,128)(2,1)} %collective-permute-done.7.refs_3_), channel_id=1, source_target_pairs={{0,4},{4,8},{8,12},{12,16},{16,20},{20,24},{24,28},{28,32},{32,36}... | collective-permute-start | bytes 2654216 | tf_op jit(solution)/shard_map/ppermute | solution.py:20
  106.7 4.9 %text_side_2.1.refs_1_ = f32[384,1152]{1,0:T(8,128)S(1)} custom-call(s32[2,7]{1,0:T(2,128)S(1)} %pad_add_fusion.flags, f32[2]{0:T(128)S(1)} %pad_maximum_fusion.scal, bf16[384,1152]{1,0:T(8,128)(2,1)S(1)} %get-tuple-element.32.refs_0_, f32[384,1152]{1,0:T(8,128)S(1)} %text_side_1.1.refs_1_, ...), custom_call_target="tpu_custom_call", output_to_operand_aliasing={{}: (3, {})} | custom-call | flops 1358954496 | bytes 7077888 | tf_op jit(solution)/shard_map/text_side_2/pallas_call | solution.py:123
  111.6 2.2 %collective-permute-done.8.refs_4_ = bf16[384,1152]{1,0:T(8,128)(2,1)S(1)} collective-permute-done((bf16[384,1152]{1,0:T(8,128)(2,1)S(1)}, bf16[384,1152]{1,0:T(8,128)(2,1)S(1)}, u32[]{:S(2)}, u32[]{:S(2)}) %collective-permute-start.8) | collective-permute-done | bytes 884768 | tf_op jit(solution)/shard_map/ppermute | solution.py:20
  113.8 0.0 collective-permute-done.9.refs_5_
  113.8 0.0 copy-done.1
  113.8 0.0 copy-start.3
  113.8 2.9 %image_side_3.1 = (bf16[384,1152]{1,0:T(8,128)(2,1)}, f32[32,1,128]{2,1,0:T(1,128)S(1)}) custom-call(s32[2,7]{1,0:T(2,128)S(1)} %pad_add_fusion.flags, f32[2]{0:T(128)S(1)} %pad_maximum_fusion.scal, f32[1]{0:T(128)} %get-tuple-element.36.refs_0_, bf16[384,1152]{1,0:T(8,128)(2,1)S(1)} %get-tuple-element.25.refs_1_, ...), custom_call_target="tpu_custom_call" | custom-call | flops 1358954496 | bytes 7077888 | tf_op jit(solution)/shard_map/image_side_3/pallas_call | solution.py:123
  116.7 17.7 %all_to_all.10.received = f32[32,1,128]{2,1,0:T(1,128)S(1)} all-to-all(f32[32,1,128]{2,1,0:T(1,128)S(1)} %get-tuple-element.41), channel_id=1, replica_groups=mesh['x_hi'=2,'y'=4,'z'=16,'x_lo'=2,'core'=2] {'x_hi','y','x_lo','core'}, dimensions={0} | all-to-all | bytes 32768 | tf_op jit(solution)/shard_map/all_to_all | solution.py:147
  134.4 0.6 plane_total.1
  135.0 5.4 %all-to-all-start.1 = ((f32[16,1,128]{2,1,0:T(1,128)}), f32[16,1,128]{2,1,0:T(1,128)S(1)}, u32[]{:S(2)}, u32[]{:S(2)}) async-start(f32[16,1,128]{2,1,0:T(1,128)} %plane_total.1), calls=%async_computation.1 | async-start | bytes 16384 | tf_op jit(solution)/shard_map/all_to_all | solution.py:147
  140.4 0.0 collective-permute-done.10.refs_3_
  140.4 0.0 collective-permute-done.11.refs_4_
  140.4 0.0 copy-done.3
  140.4 4.9 %text_side_3.1 = bf16[384,1152]{1,0:T(8,128)(2,1)} custom-call(s32[2,7]{1,0:T(2,128)S(1)} %pad_add_fusion.flags, f32[2]{0:T(128)S(1)} %pad_maximum_fusion.scal, bf16[384,1152]{1,0:T(8,128)(2,1)S(1)} %get-tuple-element.32.refs_0_, f32[384,1152]{1,0:T(8,128)S(1)} %text_side_2.1.refs_1_, bf16[384,1152]{1,0:T(8,128)(2,1)S(1)} %copy-done.3, ...), custom_call_target="tpu_custom_call" | custom-call | flops 1358954496 | bytes 7077888 | tf_op jit(solution)/shard_map/text_side_3/pallas_call | solution.py:123
  145.3 6.2 %all-to-all-done.1 = f32[16,1,128]{2,1,0:T(1,128)S(1)} async-done(((f32[16,1,128]{2,1,0:T(1,128)}), f32[16,1,128]{2,1,0:T(1,128)S(1)}, u32[]{:S(2)}, u32[]{:S(2)}) %all-to-all-start.1) | async-done | bytes 8224 | tf_op jit(solution)/shard_map/all_to_all | solution.py:147
  151.5 0.6 slice_reduce_fusion
  (4 shorter events, 0.0 us)
Async XLA Ops:
  0.6 38.4 %collective-permute-start.1 = (bf16[384,1152]{1,0:T(8,128)(2,1)}, bf16[384,1152]{1,0:T(8,128)(2,1)}, u32[]{:S(2)}, u32[]{:S(2)}) collective-permute-start(bf16[384,1152]{1,0:T(8,128)(2,1)} %refs_2_.1), channel_id=1, source_target_pairs={{0,4},{4,8},{8,12},{12,16},{16,20},{20,24},{24,28},{28,32},{32,36}... | collective-permute-start | bytes 2654216 | tf_op jit(solution)/shard_map/ppermute | solution.py:20
  5.0 34.0 %collective-permute-start = (bf16[384,1152]{1,0:T(8,128)(2,1)}, bf16[384,1152]{1,0:T(8,128)(2,1)}, u32[]{:S(2)}, u32[]{:S(2)}) collective-permute-start(bf16[384,1152]{1,0:T(8,128)(2,1)} %refs_2_.1), channel_id=1, source_target_pairs={{0,508},{4,0},{8,4},{12,8},{16,12},{20,16},{24,20},{28,24},{32,28}... | collective-permute-start | bytes 2654216 | tf_op jit(solution)/shard_map/ppermute | solution.py:20
  19.4 36.6 %collective-permute-start.5 = (bf16[384,1152]{1,0:T(8,128)(2,1)}, bf16[384,1152]{1,0:T(8,128)(2,1)S(1)}, u32[]{:S(2)}, u32[]{:S(2)}) collective-permute-start(bf16[384,1152]{1,0:T(8,128)(2,1)} %refs_3_.1), channel_id=1, source_target_pairs={{0,4},{4,8},{8,12},{12,16},{16,20},{20,24},{24,28},{28,32},{32,36}... | collective-permute-start | bytes 2654216 | tf_op jit(solution)/shard_map/ppermute | solution.py:20
  21.4 36.6 %collective-permute-start.4 = (bf16[384,1152]{1,0:T(8,128)(2,1)}, bf16[384,1152]{1,0:T(8,128)(2,1)}, u32[]{:S(2)}, u32[]{:S(2)}) collective-permute-start(bf16[384,1152]{1,0:T(8,128)(2,1)} %refs_3_.1), channel_id=1, source_target_pairs={{0,508},{4,0},{8,4},{12,8},{16,12},{20,16},{24,20},{28,24},{32,28}... | collective-permute-start | bytes 2654216 | tf_op jit(solution)/shard_map/ppermute | solution.py:20
  32.8 1.2 copy-start
  34.0 1.2 copy-start.2
  35.2 0.7 copy-start.4
  39.1 36.9 %collective-permute-start.2 = (bf16[384,1152]{1,0:T(8,128)(2,1)}, bf16[384,1152]{1,0:T(8,128)(2,1)S(1)}, u32[]{:S(2)}, u32[]{:S(2)}) collective-permute-start(bf16[384,1152]{1,0:T(8,128)(2,1)} %collective-permute-done.refs_3_), channel_id=1, source_target_pairs={{0,508},{4,0},{8,4},{12,8},{16,12},{20,16},{24,20},{28,24},{32,28}... | collective-permute-start | bytes 2654216 | tf_op jit(solution)/shard_map/ppermute | solution.py:20
  47.9 26.0 %collective-permute-start.3 = (bf16[384,1152]{1,0:T(8,128)(2,1)}, bf16[384,1152]{1,0:T(8,128)(2,1)S(1)}, u32[]{:S(2)}, u32[]{:S(2)}) collective-permute-start(bf16[384,1152]{1,0:T(8,128)(2,1)} %collective-permute-done.1.refs_4_), channel_id=1, source_target_pairs={{0,4},{4,8},{8,12},{12,16},{16,20},{20,24},{24,28},{28,32},{32,36}... | collective-permute-start | bytes 2654216 | tf_op jit(solution)/shard_map/ppermute | solution.py:20
  56.0 36.9 %collective-permute-start.7 = (bf16[384,1152]{1,0:T(8,128)(2,1)S(1)}, bf16[384,1152]{1,0:T(8,128)(2,1)}, u32[]{:S(2)}, u32[]{:S(2)}) collective-permute-start(bf16[384,1152]{1,0:T(8,128)(2,1)S(1)} %collective-permute-done.5.refs_3_), channel_id=1, source_target_pairs={{0,4},{4,8},{8,12},{12,16},{16,20},{20,24},{24,28},{28,32},{32,36}... | collective-permute-start | bytes 2654216 | tf_op jit(solution)/shard_map/ppermute | solution.py:20
  58.0 37.0 %collective-permute-start.6 = (bf16[384,1152]{1,0:T(8,128)(2,1)}, bf16[384,1152]{1,0:T(8,128)(2,1)}, u32[]{:S(2)}, u32[]{:S(2)}) collective-permute-start(bf16[384,1152]{1,0:T(8,128)(2,1)} %collective-permute-done.4.refs_2_), channel_id=1, source_target_pairs={{0,508},{4,0},{8,4},{12,8},{16,12},{20,16},{24,20},{28,24},{32,28}... | collective-permute-start | bytes 2654216 | tf_op jit(solution)/shard_map/ppermute | solution.py:20
  76.0 37.8 %collective-permute-start.8 = (bf16[384,1152]{1,0:T(8,128)(2,1)S(1)}, bf16[384,1152]{1,0:T(8,128)(2,1)S(1)}, u32[]{:S(2)}, u32[]{:S(2)}) collective-permute-start(bf16[384,1152]{1,0:T(8,128)(2,1)S(1)} %collective-permute-done.2.refs_3_), channel_id=1, source_target_pairs={{0,508},{4,0},{8,4},{12,8},{16,12},{20,16},{24,20},{28,24},{32,28}... | collective-permute-start | bytes 2654216 | tf_op jit(solution)/shard_map/ppermute | solution.py:20
  85.7 28.1 %collective-permute-start.9 = (bf16[384,1152]{1,0:T(8,128)(2,1)S(1)}, bf16[384,1152]{1,0:T(8,128)(2,1)S(1)}, u32[]{:S(2)}, u32[]{:S(2)}) collective-permute-start(bf16[384,1152]{1,0:T(8,128)(2,1)S(1)} %collective-permute-done.3.refs_4_), channel_id=1, source_target_pairs={{0,4},{4,8},{8,12},{12,16},{16,20},{20,24},{24,28},{28,32},{32,36}... | collective-permute-start | bytes 2654216 | tf_op jit(solution)/shard_map/ppermute | solution.py:20
  92.9 20.9 %copy-start.1 = (bf16[384,1152]{1,0:T(8,128)(2,1)S(1)}, bf16[384,1152]{1,0:T(8,128)(2,1)}, u32[]{:S(2)}) copy-start(bf16[384,1152]{1,0:T(8,128)(2,1)} %refs_3_.1) | copy-start | bytes 2654212
  94.9 45.5 %collective-permute-start.10 = (bf16[384,1152]{1,0:T(8,128)(2,1)}, bf16[384,1152]{1,0:T(8,128)(2,1)}, u32[]{:S(2)}, u32[]{:S(2)}) collective-permute-start(bf16[384,1152]{1,0:T(8,128)(2,1)} %collective-permute-done.6.refs_2_), channel_id=1, source_target_pairs={{0,508},{4,0},{8,4},{12,8},{16,12},{20,16},{24,20},{28,24},{32,28}... | collective-permute-start | bytes 2654216 | tf_op jit(solution)/shard_map/ppermute | solution.py:20
  104.8 35.7 %collective-permute-start.11 = (bf16[384,1152]{1,0:T(8,128)(2,1)}, bf16[384,1152]{1,0:T(8,128)(2,1)}, u32[]{:S(2)}, u32[]{:S(2)}) collective-permute-start(bf16[384,1152]{1,0:T(8,128)(2,1)} %collective-permute-done.7.refs_3_), channel_id=1, source_target_pairs={{0,4},{4,8},{8,12},{12,16},{16,20},{20,24},{24,28},{28,32},{32,36}... | collective-permute-start | bytes 2654216 | tf_op jit(solution)/shard_map/ppermute | solution.py:20
  113.8 26.7 %copy-start.3 = (bf16[384,1152]{1,0:T(8,128)(2,1)S(1)}, bf16[384,1152]{1,0:T(8,128)(2,1)}, u32[]{:S(2)}) copy-start(bf16[384,1152]{1,0:T(8,128)(2,1)} %refs_2_.1) | copy-start | bytes 2654212
  135.0 16.5 %all-to-all-start.1 = ((f32[16,1,128]{2,1,0:T(1,128)}), f32[16,1,128]{2,1,0:T(1,128)S(1)}, u32[]{:S(2)}, u32[]{:S(2)}) async-start(f32[16,1,128]{2,1,0:T(1,128)} %plane_total.1), calls=%async_computation.1 | async-start | bytes 16384 | tf_op jit(solution)/shard_map/all_to_all | solution.py:147

commit v3 on v2

--- a/solution.py
+++ b/solution.py
@@ -85,8 +85,8 @@
             loss_out[...] = jnp.full(loss_out.shape, loss[0], jnp.float32)
 
 
-def total_kernel(received, out):
-    out[...] = jnp.broadcast_to(jnp.sum(received[...], axis=0, keepdims=True), out.shape)
+def total_kernel(scale, received, out):
+    out[...] = jnp.broadcast_to(scale * jnp.sum(received[...], axis=0, keepdims=True), out.shape)
 
 
 SMEM = pl.BlockSpec(memory_space=pltpu.SMEM)
@@ -147,9 +147,9 @@
     return lax.all_to_all(values, axes, 0, 0, tiled=True)
 
 
-def totals(received, copies):
+def totals(received, copies, scale):
     return pl.pallas_call(
-        total_kernel,
+        functools.partial(total_kernel, scale),
         out_shape=jax.ShapeDtypeStruct((copies, 1, 128), jnp.float32),
         in_specs=[VMEM],
         out_specs=VMEM,
@@ -193,11 +193,11 @@
     image_grad, losses = image_side(
         3, after(loss_2, text_acc), image_acc, texts_3, image_emb, lax.axis_size(plane)
     )
-    sums = totals(exchanged(losses, plane), lax.axis_size(line))
+    images = image_emb.shape[0] * lax.axis_size(ALL)
+    sums = totals(exchanged(losses, plane), lax.axis_size(line), 1.0 / images)
     total = jnp.sum(exchanged(sums, line)[:, 0, 0]).reshape(1)
     text_grad = text_side(3, after(text_acc, sums), images_3, "3", text_emb)
-    image_count = image_emb.shape[0] * lax.axis_size(ALL)
-    return image_grad, text_grad, total / image_count
+    return image_grad, text_grad, total
 
 
 def solution(mesh):

time: 155 us -> 154 us (level)
  blocking collectives: 17.7 us -> 15.9 us
  between operations: 3.98 us -> 2.2 us
    all_to_all x1, blocking collectives: 17.7 us -> 15.9 us  [exchanged(): return lax.all_to_all(values, axes, 0, 0, tiled=True)]
    ppermute x12, waiting for transfers between devices: 16.4 us -> 18 us  [shifted(): lax.ppermute(value, axis, [(s, (s + steps) % count) for s in range(count)])]
where the time goes in v3:
time: 154 us; the launch traced here: 153 us
  starting transfers between devices  81 us (53%)
  Pallas kernels  25 us (16%)
  waiting for transfers between devices  24.1 us (16%)
  blocking collectives  15.9 us (10%)
  local copies, waits for them, and re-layouts  3.02 us (2%)
  between operations  2.2 us (1%)
  other arithmetic  1.63 us (1%)
    ppermute x12, starting transfers between devices, shifted(): lax.ppermute(value, axis, [(s, (s + steps) % count) for s in range(count)])  74.9 us
    pallas_call x6, Pallas kernels, add_pairs(): pl.pallas_call(functools.partial(pair_kernel, tuple(which), with_loss, la...  21.1 us
    ppermute x12, waiting for transfers between devices, shifted(): lax.ppermute(value, axis, [(s, (s + steps) % count) for s in range(count)])  18 us
    all_to_all x1, blocking collectives, exchanged(): return lax.all_to_all(values, axes, 0, 0, tiled=True)  15.9 us
    all_to_all x1, waiting for transfers between devices, exchanged(): return lax.all_to_all(values, axes, 0, 0, tiled=True)  6.17 us
    all_to_all x1, starting transfers between devices, exchanged(): return lax.all_to_all(values, axes, 0, 0, tiled=True)  6.15 us
    pallas_call x1, Pallas kernels, own_pair(): pl.pallas_call(own_kernel, out_shape=[jax.ShapeDtypeStruct(shape, jnp.bfl...  3.19 us
  transfers between devices with their start and end apart: 13, of which 7 were waited for; matrix products, arithmetic and copies ran while one was open for 1% of the time, Pallas kernels for 16%

profile of v3, /device:TPU:1, one launch (start us, length us, event | category | flops | bytes accessed | tf_op | source)
XLA Modules:
  0.0 152.9 jit_solution(18068269088192601796)
XLA Ops:
  0.6 4.4 %collective-permute-start.1 = (bf16[384,1152]{1,0:T(8,128)(2,1)}, bf16[384,1152]{1,0:T(8,128)(2,1)}, u32[]{:S(2)}, u32[]{:S(2)}) collective-permute-start(bf16[384,1152]{1,0:T(8,128)(2,1)} %refs_2_.1), channel_id=1, source_target_pairs={{0,4},{4,8},{8,12},{12,16},{16,20},{20,24},{24,28},{28,32},{32,36}... | collective-permute-start | bytes 2654216 | tf_op jit(solution)/shard_map/ppermute | solution.py:20
  5.0 14.4 %collective-permute-start = (bf16[384,1152]{1,0:T(8,128)(2,1)}, bf16[384,1152]{1,0:T(8,128)(2,1)}, u32[]{:S(2)}, u32[]{:S(2)}) collective-permute-start(bf16[384,1152]{1,0:T(8,128)(2,1)} %refs_2_.1), channel_id=1, source_target_pairs={{0,508},{4,0},{8,4},{12,8},{16,12},{20,16},{24,20},{28,24},{32,28}... | collective-permute-start | bytes 2654216 | tf_op jit(solution)/shard_map/ppermute | solution.py:20
  19.4 1.9 %collective-permute-start.5 = (bf16[384,1152]{1,0:T(8,128)(2,1)}, bf16[384,1152]{1,0:T(8,128)(2,1)S(1)}, u32[]{:S(2)}, u32[]{:S(2)}) collective-permute-start(bf16[384,1152]{1,0:T(8,128)(2,1)} %refs_3_.1), channel_id=1, source_target_pairs={{0,4},{4,8},{8,12},{12,16},{16,20},{20,24},{24,28},{28,32},{32,36}... | collective-permute-start | bytes 2654216 | tf_op jit(solution)/shard_map/ppermute | solution.py:20
  21.4 9.1 %collective-permute-start.4 = (bf16[384,1152]{1,0:T(8,128)(2,1)}, bf16[384,1152]{1,0:T(8,128)(2,1)}, u32[]{:S(2)}, u32[]{:S(2)}) collective-permute-start(bf16[384,1152]{1,0:T(8,128)(2,1)} %refs_3_.1), channel_id=1, source_target_pairs={{0,508},{4,0},{8,4},{12,8},{16,12},{20,16},{24,20},{28,24},{32,28}... | collective-permute-start | bytes 2654216 | tf_op jit(solution)/shard_map/ppermute | solution.py:20
  31.8 0.1 pad_maximum_fusion.scal
  31.9 0.9 select_reduce_fusion.1
  32.8 0.0 copy-start
  32.8 1.2 copy-done
  34.0 0.0 copy-start.2
  34.0 1.2 copy-done.2
  35.2 0.0 copy-start.4
  35.2 0.7 copy-done.4
  35.8 3.2 %own_pair.1 = (bf16[384,1152]{1,0:T(8,128)(2,1)S(1)}, bf16[384,1152]{1,0:T(8,128)(2,1)S(1)}, f32[384,1152]{1,0:T(8,128)S(1)}, f32[384,1152]{1,0:T(8,128)S(1)}, f32[1]{0:T(128)}) custom-call(f32[2]{0:T(128)S(1)} %pad_maximum_fusion.scal, s32[1,384]{1,0:T(1,128)S(1)} %copy-done.4, bf16[384,1152]{1,0:T(8,128)(2,1)S(1)} %copy-done, bf16[384,1152]{1,0:T(8,128)(2,1)S(1)} %copy-done.2), custom_call_target="tpu_custom_call" | custom-call | flops 1358954496 | bytes 7077888 | tf_op jit(solution)/shard_map/own_pair/pallas_call | solution.py:102
  39.0 0.0 collective-permute-done.1.refs_4_
  39.1 0.0 collective-permute-done.refs_3_
  39.1 8.8 %collective-permute-start.2 = (bf16[384,1152]{1,0:T(8,128)(2,1)}, bf16[384,1152]{1,0:T(8,128)(2,1)S(1)}, u32[]{:S(2)}, u32[]{:S(2)}) collective-permute-start(bf16[384,1152]{1,0:T(8,128)(2,1)} %collective-permute-done.refs_3_), channel_id=1, source_target_pairs={{0,508},{4,0},{8,4},{12,8},{16,12},{20,16},{24,20},{28,24},{32,28}... | collective-permute-start | bytes 2654216 | tf_op jit(solution)/shard_map/ppermute | solution.py:20
  47.9 1.9 %collective-permute-start.3 = (bf16[384,1152]{1,0:T(8,128)(2,1)}, bf16[384,1152]{1,0:T(8,128)(2,1)S(1)}, u32[]{:S(2)}, u32[]{:S(2)}) collective-permute-start(bf16[384,1152]{1,0:T(8,128)(2,1)} %collective-permute-done.1.refs_4_), channel_id=1, source_target_pairs={{0,4},{4,8},{8,12},{12,16},{16,20},{20,24},{24,28},{28,32},{32,36}... | collective-permute-start | bytes 2654216 | tf_op jit(solution)/shard_map/ppermute | solution.py:20
  49.8 4.7 %image_side_1.1 = (f32[384,1152]{1,0:T(8,128)S(1)}, f32[1]{0:T(128)}) custom-call(s32[2,7]{1,0:T(2,128)S(1)} %pad_add_fusion.flags, f32[2]{0:T(128)S(1)} %pad_maximum_fusion.scal, f32[1]{0:T(128)} %get-tuple-element.24.refs_0_, bf16[384,1152]{1,0:T(8,128)(2,1)S(1)} %get-tuple-element.25.refs_1_, ...), custom_call_target="tpu_custom_call", output_to_operand_aliasing={{0}: (4, {})} | custom-call | flops 1358954496 | bytes 7077888 | tf_op jit(solution)/shard_map/image_side_1/pallas_call | solution.py:123
  54.5 1.5 %collective-permute-done.5.refs_3_ = bf16[384,1152]{1,0:T(8,128)(2,1)S(1)} collective-permute-done((bf16[384,1152]{1,0:T(8,128)(2,1)}, bf16[384,1152]{1,0:T(8,128)(2,1)S(1)}, u32[]{:S(2)}, u32[]{:S(2)}) %collective-permute-start.5) | collective-permute-done | bytes 884768 | tf_op jit(solution)/shard_map/ppermute | solution.py:20
  56.0 1.9 %collective-permute-start.7 = (bf16[384,1152]{1,0:T(8,128)(2,1)S(1)}, bf16[384,1152]{1,0:T(8,128)(2,1)}, u32[]{:S(2)}, u32[]{:S(2)}) collective-permute-start(bf16[384,1152]{1,0:T(8,128)(2,1)S(1)} %collective-permute-done.5.refs_3_), channel_id=1, source_target_pairs={{0,4},{4,8},{8,12},{12,16},{16,20},{20,24},{24,28},{28,32},{32,36}... | collective-permute-start | bytes 2654216 | tf_op jit(solution)/shard_map/ppermute | solution.py:20
  58.0 0.0 collective-permute-done.4.refs_2_
  58.0 9.1 %collective-permute-start.6 = (bf16[384,1152]{1,0:T(8,128)(2,1)}, bf16[384,1152]{1,0:T(8,128)(2,1)}, u32[]{:S(2)}, u32[]{:S(2)}) collective-permute-start(bf16[384,1152]{1,0:T(8,128)(2,1)} %collective-permute-done.4.refs_2_), channel_id=1, source_target_pairs={{0,508},{4,0},{8,4},{12,8},{16,12},{20,16},{24,20},{28,24},{32,28}... | collective-permute-start | bytes 2654216 | tf_op jit(solution)/shard_map/ppermute | solution.py:20
  67.1 3.0 %text_side_1.1.refs_1_ = f32[384,1152]{1,0:T(8,128)S(1)} custom-call(s32[2,7]{1,0:T(2,128)S(1)} %pad_add_fusion.flags, f32[2]{0:T(128)S(1)} %pad_maximum_fusion.scal, bf16[384,1152]{1,0:T(8,128)(2,1)S(1)} %get-tuple-element.32.refs_0_, f32[384,1152]{1,0:T(8,128)S(1)} %get-tuple-element.33.refs_1_, ...), custom_call_target="tpu_custom_call", output_to_operand_aliasing={{}: (3, {})} | custom-call | flops 1358954496 | bytes 7077888 | tf_op jit(solution)/shard_map/text_side_1/pallas_call | solution.py:123
  70.1 3.8 %collective-permute-done.3.refs_4_ = bf16[384,1152]{1,0:T(8,128)(2,1)S(1)} collective-permute-done((bf16[384,1152]{1,0:T(8,128)(2,1)}, bf16[384,1152]{1,0:T(8,128)(2,1)S(1)}, u32[]{:S(2)}, u32[]{:S(2)}) %collective-permute-start.3) | collective-permute-done | bytes 884768 | tf_op jit(solution)/shard_map/ppermute | solution.py:20
  73.9 2.1 %collective-permute-done.2.refs_3_ = bf16[384,1152]{1,0:T(8,128)(2,1)S(1)} collective-permute-done((bf16[384,1152]{1,0:T(8,128)(2,1)}, bf16[384,1152]{1,0:T(8,128)(2,1)S(1)}, u32[]{:S(2)}, u32[]{:S(2)}) %collective-permute-start.2) | collective-permute-done | bytes 884768 | tf_op jit(solution)/shard_map/ppermute | solution.py:20
  76.0 9.7 %collective-permute-start.8 = (bf16[384,1152]{1,0:T(8,128)(2,1)S(1)}, bf16[384,1152]{1,0:T(8,128)(2,1)S(1)}, u32[]{:S(2)}, u32[]{:S(2)}) collective-permute-start(bf16[384,1152]{1,0:T(8,128)(2,1)S(1)} %collective-permute-done.2.refs_3_), channel_id=1, source_target_pairs={{0,508},{4,0},{8,4},{12,8},{16,12},{20,16},{24,20},{28,24},{32,28}... | collective-permute-start | bytes 2654216 | tf_op jit(solution)/shard_map/ppermute | solution.py:20
  85.7 1.9 %collective-permute-start.9 = (bf16[384,1152]{1,0:T(8,128)(2,1)S(1)}, bf16[384,1152]{1,0:T(8,128)(2,1)S(1)}, u32[]{:S(2)}, u32[]{:S(2)}) collective-permute-start(bf16[384,1152]{1,0:T(8,128)(2,1)S(1)} %collective-permute-done.3.refs_4_), channel_id=1, source_target_pairs={{0,4},{4,8},{8,12},{12,16},{16,20},{20,24},{24,28},{28,32},{32,36}... | collective-permute-start | bytes 2654216 | tf_op jit(solution)/shard_map/ppermute | solution.py:20
  87.6 2.1 %image_side_2.1 = (f32[384,1152]{1,0:T(8,128)S(1)}, f32[1]{0:T(128)}) custom-call(s32[2,7]{1,0:T(2,128)S(1)} %pad_add_fusion.flags, f32[2]{0:T(128)S(1)} %pad_maximum_fusion.scal, f32[1]{0:T(128)} %get-tuple-element.27.refs_0_, bf16[384,1152]{1,0:T(8,128)(2,1)S(1)} %get-tuple-element.25.refs_1_, ...), custom_call_target="tpu_custom_call", output_to_operand_aliasing={{0}: (4, {})} | custom-call | flops 1358954496 | bytes 7077888 | tf_op jit(solution)/shard_map/image_side_2/pallas_call | solution.py:123
  89.8 3.2 %collective-permute-done.7.refs_3_ = bf16[384,1152]{1,0:T(8,128)(2,1)} collective-permute-done((bf16[384,1152]{1,0:T(8,128)(2,1)S(1)}, bf16[384,1152]{1,0:T(8,128)(2,1)}, u32[]{:S(2)}, u32[]{:S(2)}) %collective-permute-start.7) | collective-permute-done | bytes 884768 | tf_op jit(solution)/shard_map/ppermute | solution.py:20
  92.9 0.0 copy-start.1
  92.9 2.0 %collective-permute-done.6.refs_2_ = bf16[384,1152]{1,0:T(8,128)(2,1)} collective-permute-done((bf16[384,1152]{1,0:T(8,128)(2,1)}, bf16[384,1152]{1,0:T(8,128)(2,1)}, u32[]{:S(2)}, u32[]{:S(2)}) %collective-permute-start.6) | collective-permute-done | bytes 884768 | tf_op jit(solution)/shard_map/ppermute | solution.py:20
  94.9 9.8 %collective-permute-start.10 = (bf16[384,1152]{1,0:T(8,128)(2,1)}, bf16[384,1152]{1,0:T(8,128)(2,1)}, u32[]{:S(2)}, u32[]{:S(2)}) collective-permute-start(bf16[384,1152]{1,0:T(8,128)(2,1)} %collective-permute-done.6.refs_2_), channel_id=1, source_target_pairs={{0,508},{4,0},{8,4},{12,8},{16,12},{20,16},{24,20},{28,24},{32,28}... | collective-permute-start | bytes 2654216 | tf_op jit(solution)/shard_map/ppermute | solution.py:20
  104.8 1.9 %collective-permute-start.11 = (bf16[384,1152]{1,0:T(8,128)(2,1)}, bf16[384,1152]{1,0:T(8,128)(2,1)}, u32[]{:S(2)}, u32[]{:S(2)}) collective-permute-start(bf16[384,1152]{1,0:T(8,128)(2,1)} %collective-permute-done.7.refs_3_), channel_id=1, source_target_pairs={{0,4},{4,8},{8,12},{12,16},{16,20},{20,24},{24,28},{28,32},{32,36}... | collective-permute-start | bytes 2654216 | tf_op jit(solution)/shard_map/ppermute | solution.py:20
  106.7 1.7 %text_side_2.1.refs_1_ = f32[384,1152]{1,0:T(8,128)S(1)} custom-call(s32[2,7]{1,0:T(2,128)S(1)} %pad_add_fusion.flags, f32[2]{0:T(128)S(1)} %pad_maximum_fusion.scal, bf16[384,1152]{1,0:T(8,128)(2,1)S(1)} %get-tuple-element.32.refs_0_, f32[384,1152]{1,0:T(8,128)S(1)} %text_side_1.1.refs_1_, ...), custom_call_target="tpu_custom_call", output_to_operand_aliasing={{}: (3, {})} | custom-call | flops 1358954496 | bytes 7077888 | tf_op jit(solution)/shard_map/text_side_2/pallas_call | solution.py:123
  108.4 5.4 %collective-permute-done.8.refs_4_ = bf16[384,1152]{1,0:T(8,128)(2,1)S(1)} collective-permute-done((bf16[384,1152]{1,0:T(8,128)(2,1)S(1)}, bf16[384,1152]{1,0:T(8,128)(2,1)S(1)}, u32[]{:S(2)}, u32[]{:S(2)}) %collective-permute-start.8) | collective-permute-done | bytes 884768 | tf_op jit(solution)/shard_map/ppermute | solution.py:20
  113.8 0.0 collective-permute-done.9.refs_5_
  113.8 0.0 copy-done.1
  113.8 0.0 copy-start.3
  113.8 4.7 %image_side_3.1 = (bf16[384,1152]{1,0:T(8,128)(2,1)}, f32[32,1,128]{2,1,0:T(1,128)S(1)}) custom-call(s32[2,7]{1,0:T(2,128)S(1)} %pad_add_fusion.flags, f32[2]{0:T(128)S(1)} %pad_maximum_fusion.scal, f32[1]{0:T(128)} %get-tuple-element.36.refs_0_, bf16[384,1152]{1,0:T(8,128)(2,1)S(1)} %get-tuple-element.25.refs_1_, ...), custom_call_target="tpu_custom_call" | custom-call | flops 1358954496 | bytes 7077888 | tf_op jit(solution)/shard_map/image_side_3/pallas_call | solution.py:123
  118.5 15.9 %all_to_all.10.received = f32[32,1,128]{2,1,0:T(1,128)S(1)} all-to-all(f32[32,1,128]{2,1,0:T(1,128)S(1)} %get-tuple-element.41), channel_id=1, replica_groups=mesh['x_hi'=2,'y'=4,'z'=16,'x_lo'=2,'core'=2] {'x_hi','y','x_lo','core'}, dimensions={0} | all-to-all | bytes 32768 | tf_op jit(solution)/shard_map/all_to_all | solution.py:147
  134.4 0.6 plane_total.1
  135.0 6.1 %all-to-all-start.1 = ((f32[16,1,128]{2,1,0:T(1,128)}), f32[16,1,128]{2,1,0:T(1,128)S(1)}, u32[]{:S(2)}, u32[]{:S(2)}) async-start(f32[16,1,128]{2,1,0:T(1,128)} %plane_total.1), calls=%async_computation.1 | async-start | bytes 16384 | tf_op jit(solution)/shard_map/all_to_all | solution.py:147
  141.2 0.0 collective-permute-done.10.refs_3_
  141.2 0.0 collective-permute-done.11.refs_4_
  141.2 0.0 copy-done.3
  141.2 4.9 %text_side_3.1 = bf16[384,1152]{1,0:T(8,128)(2,1)} custom-call(s32[2,7]{1,0:T(2,128)S(1)} %pad_add_fusion.flags, f32[2]{0:T(128)S(1)} %pad_maximum_fusion.scal, bf16[384,1152]{1,0:T(8,128)(2,1)S(1)} %get-tuple-element.32.refs_0_, f32[384,1152]{1,0:T(8,128)S(1)} %text_side_2.1.refs_1_, bf16[384,1152]{1,0:T(8,128)(2,1)S(1)} %copy-done.3, ...), custom_call_target="tpu_custom_call" | custom-call | flops 1358954496 | bytes 7077888 | tf_op jit(solution)/shard_map/text_side_3/pallas_call | solution.py:123
  146.1 6.2 %all-to-all-done.1 = f32[16,1,128]{2,1,0:T(1,128)S(1)} async-done(((f32[16,1,128]{2,1,0:T(1,128)}), f32[16,1,128]{2,1,0:T(1,128)S(1)}, u32[]{:S(2)}, u32[]{:S(2)}) %all-to-all-start.1) | async-done | bytes 8224 | tf_op jit(solution)/shard_map/all_to_all | solution.py:147
  152.3 0.6 slice_reduce_fusion
  (4 shorter events, 0.0 us)
Async XLA Ops:
  0.6 38.4 %collective-permute-start.1 = (bf16[384,1152]{1,0:T(8,128)(2,1)}, bf16[384,1152]{1,0:T(8,128)(2,1)}, u32[]{:S(2)}, u32[]{:S(2)}) collective-permute-start(bf16[384,1152]{1,0:T(8,128)(2,1)} %refs_2_.1), channel_id=1, source_target_pairs={{0,4},{4,8},{8,12},{12,16},{16,20},{20,24},{24,28},{28,32},{32,36}... | collective-permute-start | bytes 2654216 | tf_op jit(solution)/shard_map/ppermute | solution.py:20
  5.0 34.0 %collective-permute-start = (bf16[384,1152]{1,0:T(8,128)(2,1)}, bf16[384,1152]{1,0:T(8,128)(2,1)}, u32[]{:S(2)}, u32[]{:S(2)}) collective-permute-start(bf16[384,1152]{1,0:T(8,128)(2,1)} %refs_2_.1), channel_id=1, source_target_pairs={{0,508},{4,0},{8,4},{12,8},{16,12},{20,16},{24,20},{28,24},{32,28}... | collective-permute-start | bytes 2654216 | tf_op jit(solution)/shard_map/ppermute | solution.py:20
  19.4 36.6 %collective-permute-start.5 = (bf16[384,1152]{1,0:T(8,128)(2,1)}, bf16[384,1152]{1,0:T(8,128)(2,1)S(1)}, u32[]{:S(2)}, u32[]{:S(2)}) collective-permute-start(bf16[384,1152]{1,0:T(8,128)(2,1)} %refs_3_.1), channel_id=1, source_target_pairs={{0,4},{4,8},{8,12},{12,16},{16,20},{20,24},{24,28},{28,32},{32,36}... | collective-permute-start | bytes 2654216 | tf_op jit(solution)/shard_map/ppermute | solution.py:20
  21.4 36.6 %collective-permute-start.4 = (bf16[384,1152]{1,0:T(8,128)(2,1)}, bf16[384,1152]{1,0:T(8,128)(2,1)}, u32[]{:S(2)}, u32[]{:S(2)}) collective-permute-start(bf16[384,1152]{1,0:T(8,128)(2,1)} %refs_3_.1), channel_id=1, source_target_pairs={{0,508},{4,0},{8,4},{12,8},{16,12},{20,16},{24,20},{28,24},{32,28}... | collective-permute-start | bytes 2654216 | tf_op jit(solution)/shard_map/ppermute | solution.py:20
  32.8 1.2 copy-start
  34.0 1.2 copy-start.2
  35.2 0.7 copy-start.4
  39.1 36.9 %collective-permute-start.2 = (bf16[384,1152]{1,0:T(8,128)(2,1)}, bf16[384,1152]{1,0:T(8,128)(2,1)S(1)}, u32[]{:S(2)}, u32[]{:S(2)}) collective-permute-start(bf16[384,1152]{1,0:T(8,128)(2,1)} %collective-permute-done.refs_3_), channel_id=1, source_target_pairs={{0,508},{4,0},{8,4},{12,8},{16,12},{20,16},{24,20},{28,24},{32,28}... | collective-permute-start | bytes 2654216 | tf_op jit(solution)/shard_map/ppermute | solution.py:20
  47.9 26.0 %collective-permute-start.3 = (bf16[384,1152]{1,0:T(8,128)(2,1)}, bf16[384,1152]{1,0:T(8,128)(2,1)S(1)}, u32[]{:S(2)}, u32[]{:S(2)}) collective-permute-start(bf16[384,1152]{1,0:T(8,128)(2,1)} %collective-permute-done.1.refs_4_), channel_id=1, source_target_pairs={{0,4},{4,8},{8,12},{12,16},{16,20},{20,24},{24,28},{28,32},{32,36}... | collective-permute-start | bytes 2654216 | tf_op jit(solution)/shard_map/ppermute | solution.py:20
  56.0 36.9 %collective-permute-start.7 = (bf16[384,1152]{1,0:T(8,128)(2,1)S(1)}, bf16[384,1152]{1,0:T(8,128)(2,1)}, u32[]{:S(2)}, u32[]{:S(2)}) collective-permute-start(bf16[384,1152]{1,0:T(8,128)(2,1)S(1)} %collective-permute-done.5.refs_3_), channel_id=1, source_target_pairs={{0,4},{4,8},{8,12},{12,16},{16,20},{20,24},{24,28},{28,32},{32,36}... | collective-permute-start | bytes 2654216 | tf_op jit(solution)/shard_map/ppermute | solution.py:20
  58.0 37.0 %collective-permute-start.6 = (bf16[384,1152]{1,0:T(8,128)(2,1)}, bf16[384,1152]{1,0:T(8,128)(2,1)}, u32[]{:S(2)}, u32[]{:S(2)}) collective-permute-start(bf16[384,1152]{1,0:T(8,128)(2,1)} %collective-permute-done.4.refs_2_), channel_id=1, source_target_pairs={{0,508},{4,0},{8,4},{12,8},{16,12},{20,16},{24,20},{28,24},{32,28}... | collective-permute-start | bytes 2654216 | tf_op jit(solution)/shard_map/ppermute | solution.py:20
  76.0 37.8 %collective-permute-start.8 = (bf16[384,1152]{1,0:T(8,128)(2,1)S(1)}, bf16[384,1152]{1,0:T(8,128)(2,1)S(1)}, u32[]{:S(2)}, u32[]{:S(2)}) collective-permute-start(bf16[384,1152]{1,0:T(8,128)(2,1)S(1)} %collective-permute-done.2.refs_3_), channel_id=1, source_target_pairs={{0,508},{4,0},{8,4},{12,8},{16,12},{20,16},{24,20},{28,24},{32,28}... | collective-permute-start | bytes 2654216 | tf_op jit(solution)/shard_map/ppermute | solution.py:20
  85.7 28.1 %collective-permute-start.9 = (bf16[384,1152]{1,0:T(8,128)(2,1)S(1)}, bf16[384,1152]{1,0:T(8,128)(2,1)S(1)}, u32[]{:S(2)}, u32[]{:S(2)}) collective-permute-start(bf16[384,1152]{1,0:T(8,128)(2,1)S(1)} %collective-permute-done.3.refs_4_), channel_id=1, source_target_pairs={{0,4},{4,8},{8,12},{12,16},{16,20},{20,24},{24,28},{28,32},{32,36}... | collective-permute-start | bytes 2654216 | tf_op jit(solution)/shard_map/ppermute | solution.py:20
  92.9 20.9 %copy-start.1 = (bf16[384,1152]{1,0:T(8,128)(2,1)S(1)}, bf16[384,1152]{1,0:T(8,128)(2,1)}, u32[]{:S(2)}) copy-start(bf16[384,1152]{1,0:T(8,128)(2,1)} %refs_3_.1) | copy-start | bytes 2654212
  94.9 46.3 %collective-permute-start.10 = (bf16[384,1152]{1,0:T(8,128)(2,1)}, bf16[384,1152]{1,0:T(8,128)(2,1)}, u32[]{:S(2)}, u32[]{:S(2)}) collective-permute-start(bf16[384,1152]{1,0:T(8,128)(2,1)} %collective-permute-done.6.refs_2_), channel_id=1, source_target_pairs={{0,508},{4,0},{8,4},{12,8},{16,12},{20,16},{24,20},{28,24},{32,28}... | collective-permute-start | bytes 2654216 | tf_op jit(solution)/shard_map/ppermute | solution.py:20
  104.8 36.4 %collective-permute-start.11 = (bf16[384,1152]{1,0:T(8,128)(2,1)}, bf16[384,1152]{1,0:T(8,128)(2,1)}, u32[]{:S(2)}, u32[]{:S(2)}) collective-permute-start(bf16[384,1152]{1,0:T(8,128)(2,1)} %collective-permute-done.7.refs_3_), channel_id=1, source_target_pairs={{0,4},{4,8},{8,12},{12,16},{16,20},{20,24},{24,28},{28,32},{32,36}... | collective-permute-start | bytes 2654216 | tf_op jit(solution)/shard_map/ppermute | solution.py:20
  113.8 27.4 %copy-start.3 = (bf16[384,1152]{1,0:T(8,128)(2,1)S(1)}, bf16[384,1152]{1,0:T(8,128)(2,1)}, u32[]{:S(2)}) copy-start(bf16[384,1152]{1,0:T(8,128)(2,1)} %refs_2_.1) | copy-start | bytes 2654212
  135.0 17.2 %all-to-all-start.1 = ((f32[16,1,128]{2,1,0:T(1,128)}), f32[16,1,128]{2,1,0:T(1,128)S(1)}, u32[]{:S(2)}, u32[]{:S(2)}) async-start(f32[16,1,128]{2,1,0:T(1,128)} %plane_total.1), calls=%async_computation.1 | async-start | bytes 16384 | tf_op jit(solution)/shard_map/all_to_all | solution.py:147

commit v4 on v3

--- a/solution.py
+++ b/solution.py
@@ -64,20 +64,29 @@
     loss_out = refs.pop(0) if with_loss else None
     total = refs.pop(0) if last else out
     loss = refs.pop(0) if with_loss and last else loss_out
-    total[...] = acc[...]
     if with_loss:
         loss[0] = loss_in[0]
+    so_far = acc
     for (row, column), partner in zip(which, partners):
-
-        @pl.when(flags[row, column] > 0)
-        def _(partner=partner):
+        scored = flags[row, column] > 0
+
+        @pl.when(scored)
+        def _(partner=partner, so_far=so_far):
             other = unit_of(partner[...])[0].astype(jnp.bfloat16)
             z = scal[0] * dot(half[...], other, (1, 1)) + scal[1]
             part, sigmoid = loss_and_sigmoid(z)
             if with_loss:
                 loss[0] = loss[0] + jnp.sum(part)
             slopes = (sigmoid * scal[0]).astype(jnp.bfloat16)
-            total[...] += dot(slopes, other, (1, 0))
+            total[...] = so_far[...] + dot(slopes, other, (1, 0))
+
+        if so_far is acc:
+
+            @pl.when(jnp.logical_not(scored))
+            def _():
+                total[...] = acc[...]
+
+        so_far = total
 
     if last:
         out[...] = grad_of(raw[...], total[...])

time: 154 us -> 154 us (level)
  blocking collectives: 15.9 us -> 17.7 us
    all_to_all x1, blocking collectives: 15.9 us -> 17.7 us  [exchanged(): return lax.all_to_all(values, axes, 0, 0, tiled=True)]
where the time goes in v4:
time: 154 us
  starting transfers between devices  82 us (53%)
  Pallas kernels  24.2 us (16%)
  waiting for transfers between devices  23 us (15%)
  blocking collectives  17.7 us (11%)
  local copies, waits for them, and re-layouts  3.02 us (2%)
  between operations  2.2 us (1%)
  other arithmetic  1.63 us (1%)
    ppermute x12, starting transfers between devices, shifted(): lax.ppermute(value, axis, [(s, (s + steps) % count) for s in range(count)])  74.9 us
    pallas_call x6, Pallas kernels, add_pairs(): pl.pallas_call(functools.partial(pair_kernel, tuple(which), with_loss, la...  20.4 us
    ppermute x12, waiting for transfers between devices, shifted(): lax.ppermute(value, axis, [(s, (s + steps) % count) for s in range(count)])  18.2 us
    all_to_all x1, blocking collectives, exchanged(): return lax.all_to_all(values, axes, 0, 0, tiled=True)  17.7 us
    all_to_all x1, starting transfers between devices, exchanged(): return lax.all_to_all(values, axes, 0, 0, tiled=True)  7.11 us
    all_to_all x1, waiting for transfers between devices, exchanged(): return lax.all_to_all(values, axes, 0, 0, tiled=True)  4.89 us
    pallas_call x1, Pallas kernels, own_pair(): pl.pallas_call(own_kernel, out_shape=[jax.ShapeDtypeStruct(shape, jnp.bfl...  3.19 us
  transfers between devices with their start and end apart: 13, of which 7 were waited for; matrix products, arithmetic and copies ran while one was open for 1% of the time, Pallas kernels for 16%

profile of v4, /device:TPU:1, one launch (start us, length us, event | category | flops | bytes accessed | tf_op | source)
XLA Modules:
  0.0 153.8 jit_solution(11445667277891057240)
XLA Ops:
  0.6 4.4 %collective-permute-start.1 = (bf16[384,1152]{1,0:T(8,128)(2,1)}, bf16[384,1152]{1,0:T(8,128)(2,1)}, u32[]{:S(2)}, u32[]{:S(2)}) collective-permute-start(bf16[384,1152]{1,0:T(8,128)(2,1)} %refs_2_.1), channel_id=1, source_target_pairs={{0,4},{4,8},{8,12},{12,16},{16,20},{20,24},{24,28},{28,32},{32,36}... | collective-permute-start | bytes 2654216 | tf_op jit(solution)/shard_map/ppermute | solution.py:20
  5.0 14.4 %collective-permute-start = (bf16[384,1152]{1,0:T(8,128)(2,1)}, bf16[384,1152]{1,0:T(8,128)(2,1)}, u32[]{:S(2)}, u32[]{:S(2)}) collective-permute-start(bf16[384,1152]{1,0:T(8,128)(2,1)} %refs_2_.1), channel_id=1, source_target_pairs={{0,508},{4,0},{8,4},{12,8},{16,12},{20,16},{24,20},{28,24},{32,28}... | collective-permute-start | bytes 2654216 | tf_op jit(solution)/shard_map/ppermute | solution.py:20
  19.4 1.9 %collective-permute-start.5 = (bf16[384,1152]{1,0:T(8,128)(2,1)}, bf16[384,1152]{1,0:T(8,128)(2,1)S(1)}, u32[]{:S(2)}, u32[]{:S(2)}) collective-permute-start(bf16[384,1152]{1,0:T(8,128)(2,1)} %refs_3_.1), channel_id=1, source_target_pairs={{0,4},{4,8},{8,12},{12,16},{16,20},{20,24},{24,28},{28,32},{32,36}... | collective-permute-start | bytes 2654216 | tf_op jit(solution)/shard_map/ppermute | solution.py:20
  21.4 9.1 %collective-permute-start.4 = (bf16[384,1152]{1,0:T(8,128)(2,1)}, bf16[384,1152]{1,0:T(8,128)(2,1)}, u32[]{:S(2)}, u32[]{:S(2)}) collective-permute-start(bf16[384,1152]{1,0:T(8,128)(2,1)} %refs_3_.1), channel_id=1, source_target_pairs={{0,508},{4,0},{8,4},{12,8},{16,12},{20,16},{24,20},{28,24},{32,28}... | collective-permute-start | bytes 2654216 | tf_op jit(solution)/shard_map/ppermute | solution.py:20
  31.8 0.1 pad_maximum_fusion.scal
  31.9 0.9 select_reduce_fusion.1
  32.8 0.0 copy-start
  32.8 1.2 copy-done
  34.0 0.0 copy-start.2
  34.0 1.2 copy-done.2
  35.2 0.0 copy-start.4
  35.2 0.7 copy-done.4
  35.8 3.2 %own_pair.1 = (bf16[384,1152]{1,0:T(8,128)(2,1)S(1)}, bf16[384,1152]{1,0:T(8,128)(2,1)S(1)}, f32[384,1152]{1,0:T(8,128)S(1)}, f32[384,1152]{1,0:T(8,128)S(1)}, f32[1]{0:T(128)}) custom-call(f32[2]{0:T(128)S(1)} %pad_maximum_fusion.scal, s32[1,384]{1,0:T(1,128)S(1)} %copy-done.4, bf16[384,1152]{1,0:T(8,128)(2,1)S(1)} %copy-done, bf16[384,1152]{1,0:T(8,128)(2,1)S(1)} %copy-done.2), custom_call_target="tpu_custom_call" | custom-call | flops 1358954496 | bytes 7077888 | tf_op jit(solution)/shard_map/own_pair/pallas_call | solution.py:111
  39.0 0.0 collective-permute-done.1.refs_4_
  39.1 0.0 collective-permute-done.refs_3_
  39.1 8.8 %collective-permute-start.2 = (bf16[384,1152]{1,0:T(8,128)(2,1)}, bf16[384,1152]{1,0:T(8,128)(2,1)S(1)}, u32[]{:S(2)}, u32[]{:S(2)}) collective-permute-start(bf16[384,1152]{1,0:T(8,128)(2,1)} %collective-permute-done.refs_3_), channel_id=1, source_target_pairs={{0,508},{4,0},{8,4},{12,8},{16,12},{20,16},{24,20},{28,24},{32,28}... | collective-permute-start | bytes 2654216 | tf_op jit(solution)/shard_map/ppermute | solution.py:20
  47.9 1.9 %collective-permute-start.3 = (bf16[384,1152]{1,0:T(8,128)(2,1)}, bf16[384,1152]{1,0:T(8,128)(2,1)S(1)}, u32[]{:S(2)}, u32[]{:S(2)}) collective-permute-start(bf16[384,1152]{1,0:T(8,128)(2,1)} %collective-permute-done.1.refs_4_), channel_id=1, source_target_pairs={{0,4},{4,8},{8,12},{12,16},{16,20},{20,24},{24,28},{28,32},{32,36}... | collective-permute-start | bytes 2654216 | tf_op jit(solution)/shard_map/ppermute | solution.py:20
  49.8 4.7 %image_side_1.1 = (f32[384,1152]{1,0:T(8,128)S(1)}, f32[1]{0:T(128)}) custom-call(s32[2,7]{1,0:T(2,128)S(1)} %pad_add_fusion.flags, f32[2]{0:T(128)S(1)} %pad_maximum_fusion.scal, f32[1]{0:T(128)} %get-tuple-element.24.refs_0_, bf16[384,1152]{1,0:T(8,128)(2,1)S(1)} %get-tuple-element.25.refs_1_, ...), custom_call_target="tpu_custom_call", output_to_operand_aliasing={{0}: (4, {})} | custom-call | flops 1358954496 | bytes 7077888 | tf_op jit(solution)/shard_map/image_side_1/pallas_call | solution.py:132
  54.5 1.5 collective-permute-done.5.refs_3_
  56.0 1.9 %collective-permute-start.7 = (bf16[384,1152]{1,0:T(8,128)(2,1)S(1)}, bf16[384,1152]{1,0:T(8,128)(2,1)}, u32[]{:S(2)}, u32[]{:S(2)}) collective-permute-start(bf16[384,1152]{1,0:T(8,128)(2,1)S(1)} %collective-permute-done.5.refs_3_), channel_id=1, source_target_pairs={{0,4},{4,8},{8,12},{12,16},{16,20},{20,24},{24,28},{28,32},{32,36}... | collective-permute-start | bytes 2654216 | tf_op jit(solution)/shard_map/ppermute | solution.py:20
  58.0 0.0 collective-permute-done.4.refs_2_
  58.0 9.1 %collective-permute-start.6 = (bf16[384,1152]{1,0:T(8,128)(2,1)}, bf16[384,1152]{1,0:T(8,128)(2,1)}, u32[]{:S(2)}, u32[]{:S(2)}) collective-permute-start(bf16[384,1152]{1,0:T(8,128)(2,1)} %collective-permute-done.4.refs_2_), channel_id=1, source_target_pairs={{0,508},{4,0},{8,4},{12,8},{16,12},{20,16},{24,20},{28,24},{32,28}... | collective-permute-start | bytes 2654216 | tf_op jit(solution)/shard_map/ppermute | solution.py:20
  67.1 2.8 %text_side_1.1.refs_1_ = f32[384,1152]{1,0:T(8,128)S(1)} custom-call(s32[2,7]{1,0:T(2,128)S(1)} %pad_add_fusion.flags, f32[2]{0:T(128)S(1)} %pad_maximum_fusion.scal, bf16[384,1152]{1,0:T(8,128)(2,1)S(1)} %get-tuple-element.32.refs_0_, f32[384,1152]{1,0:T(8,128)S(1)} %get-tuple-element.33.refs_1_, ...), custom_call_target="tpu_custom_call", output_to_operand_aliasing={{}: (3, {})} | custom-call | flops 1358954496 | bytes 7077888 | tf_op jit(solution)/shard_map/text_side_1/pallas_call | solution.py:132
  69.9 4.0 %collective-permute-done.3.refs_4_ = bf16[384,1152]{1,0:T(8,128)(2,1)S(1)} collective-permute-done((bf16[384,1152]{1,0:T(8,128)(2,1)}, bf16[384,1152]{1,0:T(8,128)(2,1)S(1)}, u32[]{:S(2)}, u32[]{:S(2)}) %collective-permute-start.3) | collective-permute-done | bytes 884768 | tf_op jit(solution)/shard_map/ppermute | solution.py:20
  73.9 2.1 %collective-permute-done.2.refs_3_ = bf16[384,1152]{1,0:T(8,128)(2,1)S(1)} collective-permute-done((bf16[384,1152]{1,0:T(8,128)(2,1)}, bf16[384,1152]{1,0:T(8,128)(2,1)S(1)}, u32[]{:S(2)}, u32[]{:S(2)}) %collective-permute-start.2) | collective-permute-done | bytes 884768 | tf_op jit(solution)/shard_map/ppermute | solution.py:20
  76.0 9.7 %collective-permute-start.8 = (bf16[384,1152]{1,0:T(8,128)(2,1)S(1)}, bf16[384,1152]{1,0:T(8,128)(2,1)S(1)}, u32[]{:S(2)}, u32[]{:S(2)}) collective-permute-start(bf16[384,1152]{1,0:T(8,128)(2,1)S(1)} %collective-permute-done.2.refs_3_), channel_id=1, source_target_pairs={{0,508},{4,0},{8,4},{12,8},{16,12},{20,16},{24,20},{28,24},{32,28}... | collective-permute-start | bytes 2654216 | tf_op jit(solution)/shard_map/ppermute | solution.py:20
  85.7 1.9 %collective-permute-start.9 = (bf16[384,1152]{1,0:T(8,128)(2,1)S(1)}, bf16[384,1152]{1,0:T(8,128)(2,1)S(1)}, u32[]{:S(2)}, u32[]{:S(2)}) collective-permute-start(bf16[384,1152]{1,0:T(8,128)(2,1)S(1)} %collective-permute-done.3.refs_4_), channel_id=1, source_target_pairs={{0,4},{4,8},{8,12},{12,16},{16,20},{20,24},{24,28},{28,32},{32,36}... | collective-permute-start | bytes 2654216 | tf_op jit(solution)/shard_map/ppermute | solution.py:20
  87.6 2.1 %image_side_2.1 = (f32[384,1152]{1,0:T(8,128)S(1)}, f32[1]{0:T(128)}) custom-call(s32[2,7]{1,0:T(2,128)S(1)} %pad_add_fusion.flags, f32[2]{0:T(128)S(1)} %pad_maximum_fusion.scal, f32[1]{0:T(128)} %get-tuple-element.27.refs_0_, bf16[384,1152]{1,0:T(8,128)(2,1)S(1)} %get-tuple-element.25.refs_1_, ...), custom_call_target="tpu_custom_call", output_to_operand_aliasing={{0}: (4, {})} | custom-call | flops 1358954496 | bytes 7077888 | tf_op jit(solution)/shard_map/image_side_2/pallas_call | solution.py:132
  89.8 3.2 %collective-permute-done.7.refs_3_ = bf16[384,1152]{1,0:T(8,128)(2,1)} collective-permute-done((bf16[384,1152]{1,0:T(8,128)(2,1)S(1)}, bf16[384,1152]{1,0:T(8,128)(2,1)}, u32[]{:S(2)}, u32[]{:S(2)}) %collective-permute-start.7) | collective-permute-done | bytes 884768 | tf_op jit(solution)/shard_map/ppermute | solution.py:20
  92.9 0.0 copy-start.1
  92.9 2.0 %collective-permute-done.6.refs_2_ = bf16[384,1152]{1,0:T(8,128)(2,1)} collective-permute-done((bf16[384,1152]{1,0:T(8,128)(2,1)}, bf16[384,1152]{1,0:T(8,128)(2,1)}, u32[]{:S(2)}, u32[]{:S(2)}) %collective-permute-start.6) | collective-permute-done | bytes 884768 | tf_op jit(solution)/shard_map/ppermute | solution.py:20
  94.9 9.8 %collective-permute-start.10 = (bf16[384,1152]{1,0:T(8,128)(2,1)}, bf16[384,1152]{1,0:T(8,128)(2,1)}, u32[]{:S(2)}, u32[]{:S(2)}) collective-permute-start(bf16[384,1152]{1,0:T(8,128)(2,1)} %collective-permute-done.6.refs_2_), channel_id=1, source_target_pairs={{0,508},{4,0},{8,4},{12,8},{16,12},{20,16},{24,20},{28,24},{32,28}... | collective-permute-start | bytes 2654216 | tf_op jit(solution)/shard_map/ppermute | solution.py:20
  104.8 1.9 %collective-permute-start.11 = (bf16[384,1152]{1,0:T(8,128)(2,1)}, bf16[384,1152]{1,0:T(8,128)(2,1)}, u32[]{:S(2)}, u32[]{:S(2)}) collective-permute-start(bf16[384,1152]{1,0:T(8,128)(2,1)} %collective-permute-done.7.refs_3_), channel_id=1, source_target_pairs={{0,4},{4,8},{8,12},{12,16},{16,20},{20,24},{24,28},{28,32},{32,36}... | collective-permute-start | bytes 2654216 | tf_op jit(solution)/shard_map/ppermute | solution.py:20
  106.7 1.7 %text_side_2.1.refs_1_ = f32[384,1152]{1,0:T(8,128)S(1)} custom-call(s32[2,7]{1,0:T(2,128)S(1)} %pad_add_fusion.flags, f32[2]{0:T(128)S(1)} %pad_maximum_fusion.scal, bf16[384,1152]{1,0:T(8,128)(2,1)S(1)} %get-tuple-element.32.refs_0_, f32[384,1152]{1,0:T(8,128)S(1)} %text_side_1.1.refs_1_, ...), custom_call_target="tpu_custom_call", output_to_operand_aliasing={{}: (3, {})} | custom-call | flops 1358954496 | bytes 7077888 | tf_op jit(solution)/shard_map/text_side_2/pallas_call | solution.py:132
  108.4 5.4 %collective-permute-done.8.refs_4_ = bf16[384,1152]{1,0:T(8,128)(2,1)S(1)} collective-permute-done((bf16[384,1152]{1,0:T(8,128)(2,1)S(1)}, bf16[384,1152]{1,0:T(8,128)(2,1)S(1)}, u32[]{:S(2)}, u32[]{:S(2)}) %collective-permute-start.8) | collective-permute-done | bytes 884768 | tf_op jit(solution)/shard_map/ppermute | solution.py:20
  113.8 0.0 collective-permute-done.9.refs_5_
  113.8 0.0 copy-done.1
  113.8 0.0 copy-start.3
  113.8 2.9 %image_side_3.1 = (bf16[384,1152]{1,0:T(8,128)(2,1)}, f32[32,1,128]{2,1,0:T(1,128)S(1)}) custom-call(s32[2,7]{1,0:T(2,128)S(1)} %pad_add_fusion.flags, f32[2]{0:T(128)S(1)} %pad_maximum_fusion.scal, f32[1]{0:T(128)} %get-tuple-element.36.refs_0_, bf16[384,1152]{1,0:T(8,128)(2,1)S(1)} %get-tuple-element.25.refs_1_, ...), custom_call_target="tpu_custom_call" | custom-call | flops 1358954496 | bytes 7077888 | tf_op jit(solution)/shard_map/image_side_3/pallas_call | solution.py:132
  116.7 17.7 %all_to_all.10.received = f32[32,1,128]{2,1,0:T(1,128)S(1)} all-to-all(f32[32,1,128]{2,1,0:T(1,128)S(1)} %get-tuple-element.41), channel_id=1, replica_groups=mesh['x_hi'=2,'y'=4,'z'=16,'x_lo'=2,'core'=2] {'x_hi','y','x_lo','core'}, dimensions={0} | all-to-all | bytes 32768 | tf_op jit(solution)/shard_map/all_to_all | solution.py:156
  134.4 0.6 plane_total.1
  135.0 7.1 %all-to-all-start.1 = ((f32[16,1,128]{2,1,0:T(1,128)}), f32[16,1,128]{2,1,0:T(1,128)S(1)}, u32[]{:S(2)}, u32[]{:S(2)}) async-start(f32[16,1,128]{2,1,0:T(1,128)} %plane_total.1), calls=%async_computation.1 | async-start | bytes 16384 | tf_op jit(solution)/shard_map/all_to_all | solution.py:156
  142.1 0.0 collective-permute-done.10.refs_3_
  142.2 0.0 collective-permute-done.11.refs_4_
  142.2 0.0 copy-done.3
  142.2 6.2 %text_side_3.1 = bf16[384,1152]{1,0:T(8,128)(2,1)} custom-call(s32[2,7]{1,0:T(2,128)S(1)} %pad_add_fusion.flags, f32[2]{0:T(128)S(1)} %pad_maximum_fusion.scal, bf16[384,1152]{1,0:T(8,128)(2,1)S(1)} %get-tuple-element.32.refs_0_, f32[384,1152]{1,0:T(8,128)S(1)} %text_side_2.1.refs_1_, bf16[384,1152]{1,0:T(8,128)(2,1)S(1)} %copy-done.3, ...), custom_call_target="tpu_custom_call" | custom-call | flops 1358954496 | bytes 7077888 | tf_op jit(solution)/shard_map/text_side_3/pallas_call | solution.py:132
  148.3 4.9 %all-to-all-done.1 = f32[16,1,128]{2,1,0:T(1,128)S(1)} async-done(((f32[16,1,128]{2,1,0:T(1,128)}), f32[16,1,128]{2,1,0:T(1,128)S(1)}, u32[]{:S(2)}, u32[]{:S(2)}) %all-to-all-start.1) | async-done | bytes 8224 | tf_op jit(solution)/shard_map/all_to_all | solution.py:156
  153.2 0.6 slice_reduce_fusion
  (4 shorter events, 0.0 us)
Async XLA Ops:
  0.6 38.4 %collective-permute-start.1 = (bf16[384,1152]{1,0:T(8,128)(2,1)}, bf16[384,1152]{1,0:T(8,128)(2,1)}, u32[]{:S(2)}, u32[]{:S(2)}) collective-permute-start(bf16[384,1152]{1,0:T(8,128)(2,1)} %refs_2_.1), channel_id=1, source_target_pairs={{0,4},{4,8},{8,12},{12,16},{16,20},{20,24},{24,28},{28,32},{32,36}... | collective-permute-start | bytes 2654216 | tf_op jit(solution)/shard_map/ppermute | solution.py:20
  5.0 34.0 %collective-permute-start = (bf16[384,1152]{1,0:T(8,128)(2,1)}, bf16[384,1152]{1,0:T(8,128)(2,1)}, u32[]{:S(2)}, u32[]{:S(2)}) collective-permute-start(bf16[384,1152]{1,0:T(8,128)(2,1)} %refs_2_.1), channel_id=1, source_target_pairs={{0,508},{4,0},{8,4},{12,8},{16,12},{20,16},{24,20},{28,24},{32,28}... | collective-permute-start | bytes 2654216 | tf_op jit(solution)/shard_map/ppermute | solution.py:20
  19.4 36.6 %collective-permute-start.5 = (bf16[384,1152]{1,0:T(8,128)(2,1)}, bf16[384,1152]{1,0:T(8,128)(2,1)S(1)}, u32[]{:S(2)}, u32[]{:S(2)}) collective-permute-start(bf16[384,1152]{1,0:T(8,128)(2,1)} %refs_3_.1), channel_id=1, source_target_pairs={{0,4},{4,8},{8,12},{12,16},{16,20},{20,24},{24,28},{28,32},{32,36}... | collective-permute-start | bytes 2654216 | tf_op jit(solution)/shard_map/ppermute | solution.py:20
  21.4 36.6 %collective-permute-start.4 = (bf16[384,1152]{1,0:T(8,128)(2,1)}, bf16[384,1152]{1,0:T(8,128)(2,1)}, u32[]{:S(2)}, u32[]{:S(2)}) collective-permute-start(bf16[384,1152]{1,0:T(8,128)(2,1)} %refs_3_.1), channel_id=1, source_target_pairs={{0,508},{4,0},{8,4},{12,8},{16,12},{20,16},{24,20},{28,24},{32,28}... | collective-permute-start | bytes 2654216 | tf_op jit(solution)/shard_map/ppermute | solution.py:20
  32.8 1.2 copy-start
  34.0 1.2 copy-start.2
  35.2 0.7 copy-start.4
  39.1 36.9 %collective-permute-start.2 = (bf16[384,1152]{1,0:T(8,128)(2,1)}, bf16[384,1152]{1,0:T(8,128)(2,1)S(1)}, u32[]{:S(2)}, u32[]{:S(2)}) collective-permute-start(bf16[384,1152]{1,0:T(8,128)(2,1)} %collective-permute-done.refs_3_), channel_id=1, source_target_pairs={{0,508},{4,0},{8,4},{12,8},{16,12},{20,16},{24,20},{28,24},{32,28}... | collective-permute-start | bytes 2654216 | tf_op jit(solution)/shard_map/ppermute | solution.py:20
  47.9 26.0 %collective-permute-start.3 = (bf16[384,1152]{1,0:T(8,128)(2,1)}, bf16[384,1152]{1,0:T(8,128)(2,1)S(1)}, u32[]{:S(2)}, u32[]{:S(2)}) collective-permute-start(bf16[384,1152]{1,0:T(8,128)(2,1)} %collective-permute-done.1.refs_4_), channel_id=1, source_target_pairs={{0,4},{4,8},{8,12},{12,16},{16,20},{20,24},{24,28},{28,32},{32,36}... | collective-permute-start | bytes 2654216 | tf_op jit(solution)/shard_map/ppermute | solution.py:20
  56.0 36.9 %collective-permute-start.7 = (bf16[384,1152]{1,0:T(8,128)(2,1)S(1)}, bf16[384,1152]{1,0:T(8,128)(2,1)}, u32[]{:S(2)}, u32[]{:S(2)}) collective-permute-start(bf16[384,1152]{1,0:T(8,128)(2,1)S(1)} %collective-permute-done.5.refs_3_), channel_id=1, source_target_pairs={{0,4},{4,8},{8,12},{12,16},{16,20},{20,24},{24,28},{28,32},{32,36}... | collective-permute-start | bytes 2654216 | tf_op jit(solution)/shard_map/ppermute | solution.py:20
  58.0 37.0 %collective-permute-start.6 = (bf16[384,1152]{1,0:T(8,128)(2,1)}, bf16[384,1152]{1,0:T(8,128)(2,1)}, u32[]{:S(2)}, u32[]{:S(2)}) collective-permute-start(bf16[384,1152]{1,0:T(8,128)(2,1)} %collective-permute-done.4.refs_2_), channel_id=1, source_target_pairs={{0,508},{4,0},{8,4},{12,8},{16,12},{20,16},{24,20},{28,24},{32,28}... | collective-permute-start | bytes 2654216 | tf_op jit(solution)/shard_map/ppermute | solution.py:20
  76.0 37.8 %collective-permute-start.8 = (bf16[384,1152]{1,0:T(8,128)(2,1)S(1)}, bf16[384,1152]{1,0:T(8,128)(2,1)S(1)}, u32[]{:S(2)}, u32[]{:S(2)}) collective-permute-start(bf16[384,1152]{1,0:T(8,128)(2,1)S(1)} %collective-permute-done.2.refs_3_), channel_id=1, source_target_pairs={{0,508},{4,0},{8,4},{12,8},{16,12},{20,16},{24,20},{28,24},{32,28}... | collective-permute-start | bytes 2654216 | tf_op jit(solution)/shard_map/ppermute | solution.py:20
  85.7 28.1 %collective-permute-start.9 = (bf16[384,1152]{1,0:T(8,128)(2,1)S(1)}, bf16[384,1152]{1,0:T(8,128)(2,1)S(1)}, u32[]{:S(2)}, u32[]{:S(2)}) collective-permute-start(bf16[384,1152]{1,0:T(8,128)(2,1)S(1)} %collective-permute-done.3.refs_4_), channel_id=1, source_target_pairs={{0,4},{4,8},{8,12},{12,16},{16,20},{20,24},{24,28},{28,32},{32,36}... | collective-permute-start | bytes 2654216 | tf_op jit(solution)/shard_map/ppermute | solution.py:20
  92.9 20.9 %copy-start.1 = (bf16[384,1152]{1,0:T(8,128)(2,1)S(1)}, bf16[384,1152]{1,0:T(8,128)(2,1)}, u32[]{:S(2)}) copy-start(bf16[384,1152]{1,0:T(8,128)(2,1)} %refs_3_.1) | copy-start | bytes 2654212
  94.9 47.2 %collective-permute-start.10 = (bf16[384,1152]{1,0:T(8,128)(2,1)}, bf16[384,1152]{1,0:T(8,128)(2,1)}, u32[]{:S(2)}, u32[]{:S(2)}) collective-permute-start(bf16[384,1152]{1,0:T(8,128)(2,1)} %collective-permute-done.6.refs_2_), channel_id=1, source_target_pairs={{0,508},{4,0},{8,4},{12,8},{16,12},{20,16},{24,20},{28,24},{32,28}... | collective-permute-start | bytes 2654216 | tf_op jit(solution)/shard_map/ppermute | solution.py:20
  104.8 37.4 %collective-permute-start.11 = (bf16[384,1152]{1,0:T(8,128)(2,1)}, bf16[384,1152]{1,0:T(8,128)(2,1)}, u32[]{:S(2)}, u32[]{:S(2)}) collective-permute-start(bf16[384,1152]{1,0:T(8,128)(2,1)} %collective-permute-done.7.refs_3_), channel_id=1, source_target_pairs={{0,4},{4,8},{8,12},{12,16},{16,20},{20,24},{24,28},{28,32},{32,36}... | collective-permute-start | bytes 2654216 | tf_op jit(solution)/shard_map/ppermute | solution.py:20
  113.8 28.4 %copy-start.3 = (bf16[384,1152]{1,0:T(8,128)(2,1)S(1)}, bf16[384,1152]{1,0:T(8,128)(2,1)}, u32[]{:S(2)}) copy-start(bf16[384,1152]{1,0:T(8,128)(2,1)} %refs_2_.1) | copy-start | bytes 2654212
  135.0 18.2 %all-to-all-start.1 = ((f32[16,1,128]{2,1,0:T(1,128)}), f32[16,1,128]{2,1,0:T(1,128)S(1)}, u32[]{:S(2)}, u32[]{:S(2)}) async-start(f32[16,1,128]{2,1,0:T(1,128)} %plane_total.1), calls=%async_computation.1 | async-start | bytes 16384 | tf_op jit(solution)/shard_map/all_to_all | solution.py:156
